TPU v7x, 256 devices: a whole 4x4x8 slice. The times are simulated.
256 devices in a mesh: node: 32 (over z, x), rep: 8 (over y, core).
Axes of the slice: x: 4, y: 4, z: 8, core: 2. Of those that a mesh axis runs over, the one named last changes fastest.
Arguments:
- table: bfloat16 [49152, 768], P('node'), may hold values from -6 to 6
- near_owner: int32 [2048, 26, 1], P(('node', 'rep')), may hold values from 0 to 31; in each aligned block of 208 rows (0 to 207, 208 to 415, ..., all dimensions but the last counted through in order) at most 13 rows name the same one
- near_row: int32 [2048, 26], P(('node', 'rep')), may hold values from 0 to 1535
- far_owner: int32 [2048, 375, 1], P(('node', 'rep')), may hold values from 0 to 31; in each aligned block of 3000 rows (0 to 2999, 3000 to 5999, ..., all dimensions but the last counted through in order) at most 187 rows name the same one
- far_row: int32 [2048, 375], P(('node', 'rep')), may hold values from 0 to 1535
- w_self1: bfloat16 [768, 1024], replicated, may hold values from -0.21875 to 0.21875
- w_neigh1: bfloat16 [768, 1024], replicated, may hold values from -0.875 to 0.875
- w_self2: bfloat16 [1024, 153], replicated, may hold values from -0.1875 to 0.1875
- w_neigh2: bfloat16 [1024, 153], replicated, may hold values from -1 to 1
- out_grad: bfloat16 [2048, 153], P(('node', 'rep')), may hold values from -0.29882812 to 0.29882812
Outputs:
- grad_self1: bfloat16 [768, 1024], replicated
- grad_neigh1: bfloat16 [768, 1024], replicated
- grad_self2: bfloat16 [1024, 153], replicated
- grad_neigh2: bfloat16 [1024, 153], replicated
Inputs may be any that keep to these rules, and one draw needn't show every extreme that they name: `near_owner`: among the rows of one device no owner is named more than 13 times, a bound that some block reaches. `far_owner`: among the rows of one device no owner is named more than 187 times, a bound that some block reaches.
All inputs are finite; a program needn't handle non-finite values.
Results may differ from a plain program's by a relative error of at most 0.013.
Values may be sent and summed in bfloat16 or wider, within the bound.
A program may use at most 128 MiB of HBM per device.

v0:
```python
import jax
import jax.numpy as jnp
from jax import lax
from jax.sharding import PartitionSpec as P

F1 = 25
F2 = 15


def silu_slope(value):
    sigma = 1.0 / (1.0 + jnp.exp(-value))
    return sigma * (1.0 + value * (1.0 - sigma))


def slot_of(owners, width):
    onehot = (owners[:, None] == jnp.arange(width, dtype=jnp.int32)[None, :]).astype(jnp.int32)
    ahead = jnp.cumsum(onehot, axis=0) - onehot
    return jnp.sum(ahead * onehot, axis=1)


def fetch(buffer, table):
    return lax.all_to_all(
        table[lax.all_to_all(buffer, "node", split_axis=0, concat_axis=0, tiled=True)],
        "node",
        split_axis=0,
        concat_axis=0,
        tiled=True,
    )


def group_sums(x_far, far_flat, seeds):
    grouped = far_flat.reshape(seeds, F1, F2)
    same = grouped[..., :, None] == grouped[..., None, :]
    lower = jnp.arange(F2)[None, :] < jnp.arange(F2)[:, None]
    first = jnp.logical_not(jnp.any(same & lower, axis=-1)).astype(jnp.bfloat16)
    part = jnp.einsum(
        "stkl,stld->stkd", same.astype(jnp.bfloat16), x_far, preferred_element_type=jnp.float32
    ).astype(jnp.bfloat16)
    return jnp.einsum("stk,stkd->std", first, part, preferred_element_type=jnp.float32)


def per_device(
    table, near_owner, near_row, far_owner, far_row, w_self1, w_neigh1, w_self2, w_neigh2, out_grad
):
    width = lax.axis_size("node")
    seeds = near_owner.shape[0]
    near_count = near_owner.shape[1]
    far_count = far_owner.shape[1]
    features = table.shape[1]
    hidden = w_self1.shape[1]
    cap_near = 2 * seeds * near_count // width
    cap_far = 2 * seeds * far_count // width
    near_flat = near_owner.reshape(-1)
    near_rows = near_row.reshape(-1)
    far_flat = far_owner.reshape(-1)
    far_rows = far_row.reshape(-1)
    near_slot = slot_of(near_flat, width)
    far_slot = slot_of(far_flat, width)
    stride = cap_near + cap_far
    near_pos = near_flat * stride + near_slot
    far_pos = far_flat * stride + cap_near + far_slot
    buffer = (
        jnp.zeros((width * stride,), jnp.int32)
        .at[near_pos]
        .set(near_rows)
        .at[far_pos]
        .set(far_rows)
    )
    arrived = fetch(buffer.reshape(width, stride), table).reshape(width * stride, features)
    x_near = arrived[near_pos].reshape(seeds, near_count, features)
    x_far = arrived[far_pos].reshape(seeds, F1, F2, features)
    summed = group_sums(x_far, far_flat, seeds).reshape(seeds * F1, features)
    x_seed = x_near[:, 0]
    x_one = x_near[:, 1:].reshape(seeds * F1, features)
    mean_one = (jnp.sum(x_near[:, 1:], axis=1, dtype=jnp.float32) / F1).astype(jnp.bfloat16)
    mean_two = (summed / F2).astype(jnp.bfloat16)
    pre_seed = jnp.dot(x_seed, w_self1, preferred_element_type=jnp.float32) + jnp.dot(
        mean_one, w_neigh1, preferred_element_type=jnp.float32
    )
    pre_one = jnp.dot(x_one, w_self1, preferred_element_type=jnp.float32) + jnp.dot(
        mean_two, w_neigh1, preferred_element_type=jnp.float32
    )
    h_seed = jax.nn.silu(pre_seed).astype(jnp.bfloat16)
    h_one = jax.nn.silu(pre_one).astype(jnp.bfloat16)
    mean_h = (jnp.sum(h_one.reshape(seeds, F1, hidden), axis=1, dtype=jnp.float32) / F1).astype(
        jnp.bfloat16
    )
    grad_self2 = jnp.dot(h_seed.T, out_grad, preferred_element_type=jnp.float32)
    grad_neigh2 = jnp.dot(mean_h.T, out_grad, preferred_element_type=jnp.float32)
    d_seed = jnp.dot(out_grad, w_self2.T, preferred_element_type=jnp.float32)
    d_mean = jnp.dot(out_grad, w_neigh2.T, preferred_element_type=jnp.float32)
    g_seed = (d_seed * silu_slope(pre_seed)).astype(jnp.bfloat16)
    spread = jnp.repeat(d_mean / F1, F1, axis=0)
    g_one = (spread * silu_slope(pre_one)).astype(jnp.bfloat16)
    grad_self1 = jnp.dot(x_seed.T, g_seed, preferred_element_type=jnp.float32) + jnp.dot(
        x_one.T, g_one, preferred_element_type=jnp.float32
    )
    grad_neigh1 = jnp.dot(mean_one.T, g_seed, preferred_element_type=jnp.float32) + jnp.dot(
        mean_two.T, g_one, preferred_element_type=jnp.float32
    )
    grad_self1, grad_neigh1, grad_self2, grad_neigh2 = lax.psum(
        (grad_self1, grad_neigh1, grad_self2, grad_neigh2), ("node", "rep")
    )
    return (
        grad_self1.astype(jnp.bfloat16),
        grad_neigh1.astype(jnp.bfloat16),
        grad_self2.astype(jnp.bfloat16),
        grad_neigh2.astype(jnp.bfloat16),
    )


def solution(mesh):
    in_specs = (
        P("node", None),
        P(("node", "rep"), None, None),
        P(("node", "rep"), None),
        P(("node", "rep"), None, None),
        P(("node", "rep"), None),
        P(),
        P(),
        P(),
        P(),
        P(("node", "rep"), None),
    )
    out_specs = (P(), P(), P(), P())
    return jax.shard_map(
        per_device, mesh=mesh, in_specs=in_specs, out_specs=out_specs, check_vma=False
    )
```

profile of v0, /device:TPU:1, one launch (start us, length us, event | category | flops | bytes accessed | tf_op | source)
XLA Modules:
  0.0 504.4 jit_solution(12080361841268326812)
XLA Ops:
  1.9 9.2 %reduce-window.16 = s32[32,24,128]{2,1,0:T(8,128)S(1)} reduce-window(s32[32,24,128]{2,1,0:T(8,128)S(1)} %bitcast.69, s32[]{:T(128)} %constant.13.clone.1), window={size=1x1x128 pad=0_0x0_0x127_0}, to_apply=%region_4.5 | reduce-window | flops 12484608 | bytes 786436 | tf_op jit(solution)/shard_map/reduce-window.2
  14.7 1.3 scatter_custom_fusion
  16.0 14.7 %scatter_fusion = s32[6400]{0:T(1024)S(1)} fusion(s32[6400]{0:T(1024)S(1)} %scatter_custom_fusion, s32[3000]{0:T(1024)S(1)} %bitcast.70, s32[3000]{0:T(1024)S(1)} %reshape.219), kind=kCustom, calls=%fused_computation.4 | custom fusion | bytes 48000 | tf_op jit(solution)/shard_map/scatter | solution.py:67
  30.8 20.4 %all_to_all.17 = s32[32,1,200]{2,1,0:T(1,128)S(1)} all-to-all(s32[32,1,200]{2,1,0:T(1,128)S(1)} %all_to_all.11), channel_id=1, replica_groups=mesh['node'=32,'rep'=8] {'node'}, dimensions={0} | all-to-all | bytes 51200 | tf_op jit(solution)/shard_map/all_to_all | solution.py:23
  51.4 19.5 %gather_fusion = bf16[6400,768]{1,0:T(8,128)(2,1)} fusion(bf16[1536,768]{1,0:T(8,128)(2,1)S(1)} %copy-done, s32[7168]{0:T(1024)S(1)} %pad_clamp_fusion), kind=kCustom, calls=%fused_computation | custom fusion | bytes 19686400 | tf_op jit(solution)/shard_map/gather | solution.py:23
  70.9 5.3 %all-to-all-start.1 = ((bf16[32,200,768]{2,1,0:T(8,128)(2,1)}), bf16[32,200,768]{2,1,0:T(8,128)(2,1)}, u32[]{:S(2)}, u32[]{:S(2)}) async-start(bf16[32,200,768]{2,1,0:T(8,128)(2,1)} %bitcast.66), calls=%async_computation.1 | async-start | bytes 19660800 | tf_op jit(solution)/shard_map/all_to_all | solution.py:22
  76.8 1.8 copy.24
  80.3 220.4 %all-to-all-done.1 = bf16[32,200,768]{2,1,0:T(8,128)(2,1)} async-done(((bf16[32,200,768]{2,1,0:T(8,128)(2,1)}), bf16[32,200,768]{2,1,0:T(8,128)(2,1)}, u32[]{:S(2)}, u32[]{:S(2)}) %all-to-all-start.1) | async-done | bytes 9830432 | tf_op jit(solution)/shard_map/all_to_all | solution.py:22
  300.7 6.3 %gather_fusion.1 = bf16[208,768]{1,0:T(8,128)(2,1)S(1)} fusion(bf16[6400,768]{1,0:T(8,128)(2,1)} %bitcast.10, s32[1024]{0:T(1024)S(1)} %pad_clamp_fusion.2), kind=kCustom, calls=%fused_computation.1 | custom fusion | bytes 639808 | tf_op jit(solution)/shard_map/gather | solution.py:70
  308.1 1.7 fusion.20
  309.8 1.7 convolution_add_fusion.3
  311.7 2.3 fusion.22
  314.0 2.2 fusion.18
  316.2 1.1 fusion.12
  317.3 19.6 %gather_fusion.2 = bf16[3000,768]{1,0:T(8,128)(2,1)} fusion(bf16[6400,768]{1,0:T(8,128)(2,1)} %bitcast.10, s32[3072]{0:T(1024)S(1)} %pad_clamp_fusion.1), kind=kCustom, calls=%fused_computation.2 | custom fusion | bytes 9228000 | tf_op jit(solution)/shard_map/gather | solution.py:71
  337.0 7.8 %reshape.179 = bf16[8,25,15,768]{3,2,1,0:T(8,128)(2,1)} reshape(bf16[3000,768]{1,0:T(8,128)(2,1)} %gather_fusion.2) | data formatting | bytes 9216000 | tf_op jit(solution)/shard_map/reshape | solution.py:71
  344.8 4.5 fusion
  349.5 1.1 reshape.177
  350.6 1.9 fusion.31
  352.5 3.4 fusion.6
  355.9 2.3 convolution_add_fusion
  358.5 2.3 convolution_add_fusion.1
  360.8 1.3 reshape.182
  362.5 141.9 %all-reduce.4 = (bf16[768,1024]{1,0:T(8,128)(2,1)}, bf16[768,1024]{1,0:T(8,128)(2,1)}, bf16[1024,153]{0,1:T(8,128)(2,1)}, bf16[1024,153]{0,1:T(8,128)(2,1)}) all-reduce(f32[768,1024]{1,0:T(8,128)} %convolution_add_fusion.1, f32[768,1024]{1,0:T(8,128)} %convolution_add_fusion, ...), channel_id=1, replica_groups=mesh['node'=32,'rep'=8] {'node','rep'}, use_global_device_ids=true, to_apply=%region_10.11 | all-reduce | flops 1886208 | bytes 11317248 | tf_op jit(solution)/shard_map/psum | solution.py:101
  (72 shorter events, 9.5 us)
Async XLA Ops:
  0.6 50.8 %copy-start = (bf16[1536,768]{1,0:T(8,128)(2,1)S(1)}, bf16[1536,768]{1,0:T(8,128)(2,1)}, u32[]{:S(2)}) copy-start(bf16[1536,768]{1,0:T(8,128)(2,1)} %param.10) | copy-start | bytes 7077892
  0.6 12.0 %copy-start.8 = (s32[8,26,1]{1,2,0:T(1,128)S(1)}, s32[8,26,1]{1,2,0:T(1,128)}, u32[]{:S(2)}) copy-start(s32[8,26,1]{1,2,0:T(1,128)} %param.11) | copy-start | bytes 2500
  0.7 13.8 %copy-start.9 = (s32[8,26]{1,0:T(8,128)S(1)}, s32[8,26]{1,0:T(8,128)}, u32[]{:S(2)}) copy-start(s32[8,26]{1,0:T(8,128)} %param.12) | copy-start | bytes 2500
  0.7 13.9 %copy-start.7 = (s32[8,375]{1,0:T(8,128)S(1)}, s32[8,375]{1,0:T(8,128)}, u32[]{:S(2)}) copy-start(s32[8,375]{1,0:T(8,128)} %param.14) | copy-start | bytes 36004
  70.9 8.1 %copy-start.4 = (bf16[1024,153]{0,1:T(8,128)(2,1)S(1)}, bf16[1024,153]{0,1:T(8,128)(2,1)}, u32[]{:S(2)}) copy-start(bf16[1024,153]{0,1:T(8,128)(2,1)} %param.18) | copy-start | bytes 940036
  70.9 8.1 %copy-start.6 = (bf16[8,153]{1,0:T(8,128)(2,1)S(1)}, bf16[8,153]{1,0:T(8,128)(2,1)}, u32[]{:S(2)}) copy-start(bf16[8,153]{1,0:T(8,128)(2,1)} %param.19) | copy-start | bytes 7348
  70.9 229.8 %all-to-all-start.1 = ((bf16[32,200,768]{2,1,0:T(8,128)(2,1)}), bf16[32,200,768]{2,1,0:T(8,128)(2,1)}, u32[]{:S(2)}, u32[]{:S(2)}) async-start(bf16[32,200,768]{2,1,0:T(8,128)(2,1)} %bitcast.66), calls=%async_computation.1 | async-start | bytes 19660800 | tf_op jit(solution)/shard_map/all_to_all | solution.py:22
  307.0 4.6 copy-start.5
  337.0 7.8 %copy-start.3 = (pred[8,25,15,15]{3,2,1,0:T(8,128)(4,1)S(1)}, pred[8,25,15,15]{3,2,1,0:T(8,128)(4,1)}, u32[]{:S(2)}) copy-start(pred[8,25,15,15]{3,2,1,0:T(8,128)(4,1)} %copy.24) | copy-start | bytes 135004
  352.5 3.4 copy-start.2
  355.9 2.7 copy-start.1
where the time goes:
time: 506 us; the launch traced here: 504 us
  waiting for transfers between devices  220 us (43%)
  blocking collectives  162 us (32%)
  local copies, waits for them, and re-layouts  78.6 us (16%)
  matrix products  24 us (5%)
  other arithmetic  13 us (3%)
  starting transfers between devices  5.29 us (1%)
    all_to_all x1, waiting for transfers between devices, fetch(): lax.all_to_all(table[lax.all_to_all(buffer, 'node', split_axis=0, concat_...  220 us
    psum x1, blocking collectives, per_device(): lax.psum((grad_self1, grad_neigh1, grad_self2, grad_neigh2), ('node', 're...  142 us
    all_to_all x1, blocking collectives, fetch(): lax.all_to_all(buffer, 'node', split_axis=0, concat_axis=0, tiled=True)  20.4 us
    gather x1, local copies, waits for them, and re-layouts, per_device(): x_far = arrived[far_pos].reshape(seeds, F1, F2, features)  19.6 us
    gather x1, local copies, waits for them, and re-layouts, fetch(): table[lax.all_to_all(buffer, 'node', split_axis=0, concat_axis=0, tiled=T...  19.5 us
    scatter x2, local copies, waits for them, and re-layouts, per_device(): buffer = jnp.zeros((width * stride,), jnp.int32).at[near_pos].set(near_ro...  16 us
    another operation x7, other arithmetic  10.3 us
  transfers between devices with their start and end apart: 1, of which 1 were waited for; matrix products, arithmetic and copies ran while one was open for 1% of the time, Pallas kernels for 0%

commit v1 on v0

v1 whole, which is shorter than its diff:
```python
import jax, jax.numpy as jnp
from jax import lax
from jax.sharding import PartitionSpec as P
from jax.experimental import pallas as pl
from jax.experimental.pallas import tpu as pltpu
MESH = pl.DeviceIdType.MESH
NZ, NX, REP = 8, 4, 8
ROWS, W = 1536, 96
F1, F2 = 25, 15
G4 = ROWS // 4
UNITS = ((0, 80), (80, 80), (160, 112), (272, 112))


def plan():
    msgs = []
    def hops(size, half):
        out = []
        for h in range(1, size // 2 + 1):
            for d in (1, -1):
                if 2 * h == size and (d == 1) != (half == 0):
                    continue
                out.append((h, d))
        return out
    for u in range(4):
        half = u % 2
        first, second = ("x", "z") if u < 2 else ("z", "x")
        size = {"x": NX, "z": NZ}
        reach = [(0, 0)]
        for h, d in hops(size[first], half):
            off = {first: -h * d, second: 0}
            msgs.append((h, u, off["x"], off["z"], first, d))
            reach.append((-h * d, h))
        for o, base in reach:
            for h, d in hops(size[second], half):
                off = {first: o, second: -h * d}
                msgs.append((base + h, u, off["x"], off["z"], second, d))
    msgs.sort(key=lambda m: m[0])
    return msgs


PLAN = plan()


def fetch_kernel(idx_ref, table_ref, out_ref, land, t32, sums, ones, stage, idx_land, idx_smem,
                 send_sem, recv_sem, isend, irecv, osend, orecv, lsem):
    node, rep = lax.axis_index("node"), lax.axis_index("rep")
    z, x = node // NX, node % NX

    def at(dx, dz):
        return ((z + dz + 2 * NZ) % NZ) * NX + (x + dx + 2 * NX) % NX

    barrier = pltpu.get_barrier_semaphore()
    for n in (at(1, 0), at(-1, 0), at(0, 1), at(0, -1)):
        pl.semaphore_signal(barrier, inc=1, device_id=(n, rep), device_id_type=MESH)
    for k in range(1, REP):
        pl.semaphore_signal(barrier, inc=1, device_id=(node, (rep + k) % REP), device_id_type=MESH)

    c = lax.broadcasted_iota(jnp.int32, (768, 384), 0)
    d = lax.broadcasted_iota(jnp.int32, (768, 384), 1)
    j = d // 128
    hit = c == rep * W + j * 32 + d % 32
    group = jnp.where(hit, ((d // 32) % 4 - j + 4) % 4, -1)
    acc = jnp.zeros((G4, 384), jnp.float32)
    for g in range(4):
        perm = jnp.where(group == g, 1.0, 0.0).astype(jnp.bfloat16)
        acc = acc + jnp.dot(table_ref[g * G4:(g + 1) * G4, :], perm, preferred_element_type=jnp.float32)
    land[node] = acc.astype(jnp.bfloat16)
    pl.semaphore_wait(barrier, 4 + REP - 1)

    def icopy(k):
        return pltpu.make_async_remote_copy(src_ref=idx_ref, dst_ref=idx_land.at[rep], send_sem=isend.at[k], recv_sem=irecv.at[k],
                                            device_id=(node, (rep + k) % REP), device_id_type=MESH)
    for k in range(1, REP):
        icopy(k).start()
    idx_land[rep] = idx_ref[...]

    def slot(u, n):
        return land.at[n, pl.ds(UNITS[u][0], UNITS[u][1])]

    def send(m, i):
        _, u, ox, oz, axis, dr = m
        sx, sz = (ox + dr, oz) if axis == "x" else (ox, oz + dr)
        to = at(dr, 0) if axis == "x" else at(0, dr)
        s = slot(u, at(sx, sz))
        return pltpu.make_async_remote_copy(src_ref=s, dst_ref=s, send_sem=send_sem.at[i], recv_sem=recv_sem.at[i],
                                            device_id=(to, rep), device_id_type=MESH)

    def arrival(m, i):
        _, u, ox, oz, axis, dr = m
        s = slot(u, at(ox, oz))
        return pltpu.make_async_remote_copy(src_ref=s, dst_ref=s, send_sem=send_sem.at[i], recv_sem=recv_sem.at[i],
                                            device_id=(node, (rep + 1) % REP), device_id_type=MESH)

    lane = lax.broadcasted_iota(jnp.int32, (16, 128), 1) // 32

    def unpack(n):
        def body(i, _):
            r0 = pl.multiple_of(i * 16, 16)
            p = land[n, pl.ds(r0, 16), :].astype(jnp.float32)
            ps = [p[:, 128 * q:128 * q + 128] for q in range(3)]
            for g in range(4):
                s = jnp.where(lane == g, ps[0], jnp.where(lane == (g + 1) % 4, ps[1], jnp.where(lane == (g + 2) % 4, ps[2], 0.0)))
                if g:
                    s = pltpu.roll(s, 128 - 32 * g, 1)
                t32[pl.ds(pl.multiple_of(n * ROWS + g * G4 + r0, 16), 16), :] = s
            return 0
        lax.fori_loop(0, G4 // 16, body, 0)

    def start_children(u, ox, oz, started):
        for i, m in enumerate(PLAN):
            if m[1] != u or i in started:
                continue
            sx, sz = (m[2] + m[5], m[3]) if m[4] == "x" else (m[2], m[3] + m[5])
            if (sx % NX, sz % NZ) == (ox % NX, oz % NZ):
                started.add(i)
                send(m, i).start()

    started = set()
    for u in range(4):
        start_children(u, 0, 0, started)
    last = max(m[0] for m in PLAN)
    unpack(node)
    for k in range(1, REP):
        icopy(k).wait_recv()
    cp = pltpu.make_async_copy(idx_land, idx_smem, lsem)
    cp.start()
    for t in range(1, last + 1):
        seen = []
        for i, m in enumerate(PLAN):
            if m[0] != t:
                continue
            arrival(m, i).wait_recv()
            start_children(m[1], m[2], m[3], started)
            if (m[2] % NX, m[3] % NZ) not in seen:
                seen.append((m[2] % NX, m[3] % NZ))
        for ox, oz in seen:
            unpack(at(ox, oz))
    assert len(started) == len(PLAN)
    cp.wait()

    def ocopy(k):
        return pltpu.make_async_remote_copy(src_ref=stage.at[k], dst_ref=out_ref.at[rep], send_sem=osend.at[k], recv_sem=orecv.at[k],
                                            device_id=(node, (rep + k) % REP), device_id_type=MESH)

    for k in list(range(1, REP)) + [0]:
        p = (rep + k) % REP

        def body(i, _):
            for u in range(8):
                def row(q):
                    return t32[pl.ds(idx_smem[p, i, 16 * u + q], 1), :]
                rows = [row(q) for q in range(15)]
                while len(rows) > 1:
                    rows = [rows[a] + rows[a + 1] if a + 1 < len(rows) else rows[a] for a in range(0, len(rows), 2)]
                sums[pl.ds(i * 8 + u, 1), :] = rows[0]
                ones[pl.ds(i * 8 + u, 1), :] = row(15)
            return 0
        lax.fori_loop(0, 25, body, 0)
        for u in range(8):
            ones[pl.ds(200 + u, 1), :] = t32[pl.ds(idx_smem[p, 25, u], 1), :]
        sums[200:208, :] = jnp.zeros((8, 128), jnp.float32)
        for h, part in ((0, (sums[...] / 15.0)), (1, ones[...])):
            if k:
                stage[k, 208 * h:208 * h + 208, :] = part.astype(jnp.bfloat16)
            else:
                out_ref[rep, 208 * h:208 * h + 208, :] = part.astype(jnp.bfloat16)
        if k:
            ocopy(k).start()
    for k in range(1, REP):
        ocopy(k).wait()
        icopy(k).wait_send()
    for i, m in enumerate(PLAN):
        send(m, i).wait_send()


def fetch(idx, table):
    n = len(PLAN)
    return pl.pallas_call(
        fetch_kernel,
        out_shape=jax.ShapeDtypeStruct((REP, 416, 128), jnp.bfloat16),
        in_specs=[pl.BlockSpec(memory_space=pltpu.VMEM)] * 2,
        out_specs=pl.BlockSpec(memory_space=pltpu.VMEM),
        scratch_shapes=[
            pltpu.VMEM((NZ * NX, G4, 384), jnp.bfloat16),
            pltpu.VMEM((NZ * NX * ROWS, 128), jnp.float32),
            pltpu.VMEM((208, 128), jnp.float32),
            pltpu.VMEM((208, 128), jnp.float32),
            pltpu.VMEM((REP, 416, 128), jnp.bfloat16),
            pltpu.VMEM((REP, 32, 128), jnp.int32),
            pltpu.SMEM((REP, 32, 128), jnp.int32),
            pltpu.SemaphoreType.DMA((n,)),
            pltpu.SemaphoreType.DMA((n,)),
            pltpu.SemaphoreType.DMA((REP,)),
            pltpu.SemaphoreType.DMA((REP,)),
            pltpu.SemaphoreType.DMA((REP,)),
            pltpu.SemaphoreType.DMA((REP,)),
            pltpu.SemaphoreType.DMA,
        ],
        compiler_params=pltpu.CompilerParams(collective_id=0, has_side_effects=True, vmem_limit_bytes=56 * 2**20),
        cost_estimate=pl.CostEstimate(flops=10**9, bytes_accessed=10**7, transcendentals=0),
        name="fetch",
    )(idx, table)


def build_idx(near_owner, near_row, far_owner, far_row):
    near = near_owner[..., 0] * ROWS + near_row
    far = far_owner[..., 0] * ROWS + far_row
    pairs = jnp.concatenate([far.reshape(200, 15), near[:, 1:].reshape(200, 1)], axis=1).reshape(25, 128)
    seed = jnp.pad(near[:, :1].reshape(1, 8), ((0, 0), (0, 120)))
    return jnp.concatenate([pairs, seed, jnp.zeros((6, 128), jnp.int32)], axis=0)


def silu_slope(value):
    sigma = 1.0 / (1.0 + jnp.exp(-value))
    return sigma * (1.0 + value * (1.0 - sigma))


def per_device(
    table, near_owner, near_row, far_owner, far_row, w_self1, w_neigh1, w_self2, w_neigh2, out_grad
):
    seeds, hidden = 8, w_self1.shape[1]
    got = fetch(build_idx(near_owner, near_row, far_owner, far_row), table)
    got = got[:, :, :W].transpose(1, 0, 2).reshape(416, REP * W)
    mean_two, x_one, x_seed = got[:200], got[208:408], got[408:]
    mean_one = (jnp.sum(x_one.reshape(seeds, F1, -1), axis=1, dtype=jnp.float32) / F1).astype(jnp.bfloat16)
    x_all = got[208:]
    m_all = jnp.concatenate([mean_two, mean_one], axis=0)
    pre = jnp.dot(x_all, w_self1, preferred_element_type=jnp.float32) + jnp.dot(
        m_all, w_neigh1, preferred_element_type=jnp.float32
    )
    h = jax.nn.silu(pre).astype(jnp.bfloat16)
    h_seed = h[200:]
    mean_h = (jnp.sum(h[:200].reshape(seeds, F1, hidden), axis=1, dtype=jnp.float32) / F1).astype(jnp.bfloat16)
    grad_self2 = jnp.dot(h_seed.T, out_grad, preferred_element_type=jnp.float32)
    grad_neigh2 = jnp.dot(mean_h.T, out_grad, preferred_element_type=jnp.float32)
    d_seed = jnp.dot(out_grad, w_self2.T, preferred_element_type=jnp.float32)
    d_mean = jnp.dot(out_grad, w_neigh2.T, preferred_element_type=jnp.float32)
    d_all = jnp.concatenate([jnp.repeat(d_mean / F1, F1, axis=0), d_seed], axis=0)
    g = (d_all * silu_slope(pre)).astype(jnp.bfloat16)
    grad_self1 = jnp.dot(x_all.T, g, preferred_element_type=jnp.float32)
    grad_neigh1 = jnp.dot(m_all.T, g, preferred_element_type=jnp.float32)
    grads = lax.psum((grad_self1, grad_neigh1, grad_self2, grad_neigh2), ("node", "rep"))
    return tuple(v.astype(jnp.bfloat16) for v in grads)


def solution(mesh):
    rows = P(("node", "rep"))
    return jax.shard_map(
        per_device,
        mesh=mesh,
        in_specs=(P("node"), rows, rows, rows, rows, P(), P(), P(), P(), rows),
        out_specs=(P(), P(), P(), P()),
        check_vma=False,
    )
```

time: 506 us -> 275 us (0.54)
  waiting for transfers between devices: 220 us -> 0 us
  Pallas kernels: 0 us -> 108 us
  local copies, waits for them, and re-layouts: 78.6 us -> 6.87 us
  blocking collectives: 162 us -> 140 us
  other arithmetic: 13 us -> 2.7 us
  matrix products: 24 us -> 15.6 us
  starting transfers between devices: 5.29 us -> 0 us
    all_to_all x1 -> x0, waiting for transfers between devices: 220 us -> none  [fetch(): lax.all_to_all(table[lax.all_to_all(buffer, 'node', split_axis=0, concat_...]
    pallas_call x0 -> x1, Pallas kernels: none -> 108 us  [fetch(): pl.pallas_call(fetch_kernel, out_shape=jax.ShapeDtypeStruct((REP, 416, 12...]
    gather x3 -> x0, local copies, waits for them, and re-layouts: 45.4 us -> none  [the longest x1 19.6 us: per_device(): x_far = arrived[far_pos].reshape(seeds, F1, F2, features)]
    all_to_all x1 -> x0, blocking collectives: 20.4 us -> none  [fetch(): lax.all_to_all(buffer, 'node', split_axis=0, concat_axis=0, tiled=True)]
    scatter x2 -> x0, local copies, waits for them, and re-layouts: 16 us -> none  [per_device(): buffer = jnp.zeros((width * stride,), jnp.int32).at[near_pos].set(near_ro...]
    dot_general x9 -> x4, matrix products: 22.3 us -> 11.3 us  [the longest x1 3.32 us: per_device(): grad_neigh1 = jnp.dot(m_all.T, g, preferred_element_type=jnp.float32)]
    another operation x7 -> x0, other arithmetic: 10.3 us -> none
    reshape x6 -> x4, local copies, waits for them, and re-layouts: 10.2 us -> 1.28 us  [the longest x1 1 us: per_device(): jnp.repeat(d_mean / F1, F1, axis=0)]
  transfers between devices with their start and end apart: 1 -> 0, of which waited for: 1 -> 0; matrix products, arithmetic and copies ran while one was open for 1% -> 0% of each run, Pallas kernels for 0% -> 0%
where the time goes in v1:
time: 275 us; the launch traced here: 274 us
  blocking collectives  140 us (51%)
  Pallas kernels  108 us (39%)
  matrix products  15.6 us (6%)
  local copies, waits for them, and re-layouts  6.87 us (2%)
    psum x1, blocking collectives, per_device(): lax.psum((grad_self1, grad_neigh1, grad_self2, grad_neigh2), ('node', 're...  140 us
    pallas_call x1, Pallas kernels, fetch(): pl.pallas_call(fetch_kernel, out_shape=jax.ShapeDtypeStruct((REP, 416, 12...  108 us

profile of v1, /device:TPU:1, one launch (start us, length us, event | category | flops | bytes accessed | tf_op | source)
XLA Modules:
  0.0 273.8 jit_solution(16784561883421311314)
XLA Ops:
  0.7 0.8 bitcast_add_fusion.1
  1.5 0.1 slice_reduce_fusion
  1.7 0.7 bitcast_add_fusion
  2.5 1.7 fusion.11
  4.2 1.1 convolution_multiply_fusion
  5.8 0.7 fusion.5.idx_ref
  6.4 108.0 %fetch.1 = bf16[8,416,128]{2,1,0:T(8,128)(2,1)} custom-call(s32[32,128]{1,0:T(8,128)} %fusion.5.idx_ref, bf16[1536,768]{1,0:T(8,128)(2,1)} %table_ref.1), custom_call_target="tpu_custom_call" | custom-call | flops 1000000000 | bytes 10000000 | tf_op jit(solution)/shard_map/fetch/pallas_call | solution.py:178
  114.5 1.2 slice_bitcast_fusion
  115.7 0.1 copy.44
  115.8 1.1 slice.35
  117.0 1.0 slice.37
  118.1 0.2 copy.46
  118.3 0.3 reshape.43
  118.7 0.5 copy-done.1
  119.2 2.8 %fusion.12 = f32[208,1024]{1,0:T(8,128)} fusion(bf16[208,768]{1,0:T(8,128)(2,1)S(1)} %copy-done.1, bf16[768,1024]{1,0:T(8,128)(2,1)} %param.15), kind=kOutput, calls=%fused_computation.29 | convolution fusion | flops 327155712 | bytes 2744320 | tf_op jit(solution)/shard_map/dot_general | solution.py:228
  122.1 1.0 reshape.42
  123.2 2.9 %multiply_convert_fusion = (bf16[208,1024]{1,0:T(8,128)(2,1)S(1)}, bf16[208,1024]{1,0:T(8,128)(2,1)}) fusion(f32[8,1024]{1,0:T(8,128)S(1)} %copy-done.7, f32[200,1024]{1,0:T(8,128)} %reshape.42, f32[208,1024]{1,0:T(8,128)} %fusion.12, bf16[768,1024]{1,0:T(8,128)(2,1)S(1)} %copy-done, bf16[8,768]{1,0:T(8,128)(2,1)S(1)} %multiply_convert_fusion.2, ...), kind=kOutput, calls=%fused_computation.4 | convolution fusion | flops 330563584 | bytes 4448256 | tf_op jit(solution)/shard_map/dot_general | solution.py:228
  126.1 1.1 fusion.3
  127.4 0.1 reduce_sum.19
  127.6 0.3 fusion.2
  127.9 0.6 copy-done.4
  128.4 3.3 %fusion.1 = f32[768,1024]{1,0:T(8,128)} fusion(bf16[208,1024]{1,0:T(8,128)(2,1)S(1)} %copy-done.4, bf16[8,768]{1,0:T(8,128)(2,1)S(1)} %multiply_convert_fusion.2, bf16[200,768]{1,0:T(8,128)(2,1)} %slice.37), kind=kOutput, calls=%fused_computation.10 | convolution fusion | flops 327794688 | bytes 3891200 | tf_op jit(solution)/shard_map/dot_general | solution.py:241
  131.8 2.3 fusion.13
  134.0 139.8 %all-reduce.3 = (bf16[768,1024]{1,0:T(8,128)(2,1)}, bf16[768,1024]{1,0:T(8,128)(2,1)}, bf16[1024,153]{0,1:T(8,128)(2,1)}, bf16[1024,153]{0,1:T(8,128)(2,1)}) all-reduce(f32[768,1024]{1,0:T(8,128)} %fusion.13, f32[768,1024]{1,0:T(8,128)} %fusion.1, f32[1024,153]{0,1:T(8,128)S(1)} %copy-done.3, ...), channel_id=1, replica_groups=mesh['node'=32,'rep'=8] {'node','rep'}, use_global_device_ids=true, to_apply=%region_1.2 | all-reduce | flops 1886208 | bytes 11317248 | tf_op jit(solution)/shard_map/psum | solution.py:242
  (29 shorter events, 1.1 us)
Async XLA Ops:
  0.6 122.5 %copy-start = (bf16[768,1024]{1,0:T(8,128)(2,1)S(1)}, bf16[768,1024]{1,0:T(8,128)(2,1)}, u32[]{:S(2)}) copy-start(bf16[768,1024]{1,0:T(8,128)(2,1)} %param.16) | copy-start | bytes 4718596
  118.2 1.0 copy-start.1
  122.0 1.1 copy-start.5
  122.0 1.1 copy-start.7
  123.2 2.9 %copy-start.6 = (bf16[8,153]{1,0:T(8,128)(2,1)S(1)}, bf16[8,153]{1,0:T(8,128)(2,1)}, u32[]{:S(2)}) copy-start(bf16[8,153]{1,0:T(8,128)(2,1)} %param.19) | copy-start | bytes 7348
  127.4 1.0 copy-start.4
  128.4 3.3 %copy-start.2 = (bf16[208,768]{1,0:T(8,128)(2,1)S(1)}, bf16[208,768]{1,0:T(8,128)(2,1)}, u32[]{:S(2)}) copy-start(bf16[208,768]{1,0:T(8,128)(2,1)} %slice.35) | copy-start | bytes 958468
  131.8 2.3 copy-start.3

commit v2 on v1

--- a/solution.py
+++ b/solution.py
@@ -6,7 +6,6 @@
 MESH = pl.DeviceIdType.MESH
 NZ, NX, REP = 8, 4, 8
 ROWS, W = 1536, 96
-F1, F2 = 25, 15
 G4 = ROWS // 4
 UNITS = ((0, 80), (80, 80), (160, 112), (272, 112))
 
@@ -210,37 +209,306 @@
     return jnp.concatenate([pairs, seed, jnp.zeros((6, 128), jnp.int32)], axis=0)
 
 
-def silu_slope(value):
-    sigma = 1.0 / (1.0 + jnp.exp(-value))
-    return sigma * (1.0 + value * (1.0 - sigma))
+F1 = 25
+WIDE = 256
+ROWS_G = 2048
+CP = 160
+N_SEM = 2 + 2 * (6 + 6 + 7 + 7 + 4 + 4 + 4)
+
+
+def step_kernel(got_ref, ws1, wn1, ws2, wn2, og_ref, fin, xs, ms, acc, sb, sib, crecv, big, small, tiny, send_sem, recv_sem):
+    node, rep = lax.axis_index("node"), lax.axis_index("rep")
+    z, x = node // NX, node % NX
+    y, core = rep // 2, rep % 2
+
+    def dev(axis, d):
+        if axis == "x":
+            return (z * NX + (x + d + NX) % NX, rep)
+        if axis == "y":
+            return (node, ((y + d + 4) % 4) * 2 + core)
+        if axis == "z":
+            return (((z + d + NZ) % NZ) * NX + x, rep)
+        return (node, y * 2 + 1 - core)
+
+    barrier = pltpu.get_barrier_semaphore()
+    peers = [("x", 1), ("x", -1), ("y", 1), ("y", -1), ("c", 1)] + [("z", k) for k in range(1, NZ)]
+    for a, d in peers:
+        pl.semaphore_signal(barrier, inc=1, device_id=dev(a, d), device_id_type=MESH)
+
+    counter = [0]
+
+    def new():
+        counter[0] += 1
+        return counter[0] - 1
+
+    def copy(i, src, dst, axis, d):
+        return pltpu.make_async_remote_copy(src_ref=src, dst_ref=dst, send_sem=send_sem.at[i], recv_sem=recv_sem.at[i],
+                                            device_id=dev(axis, d), device_id_type=MESH)
+    sent = []
+
+    def send(i, src, dst, axis, d):
+        c = copy(i, src, dst, axis, d)
+        c.start()
+        sent.append(c)
+
+    def arrive(i, dst):
+        copy(i, dst, dst, "c", 1).wait_recv()
+
+    for ref, lo in ((ms, 0), (xs, 208)):
+        lane = lax.broadcasted_iota(jnp.int32, (208, 128), 1)
+        chunks = [None] * 6
+        for r in range(REP):
+            q, o = 96 * r // 128, 96 * r % 128
+            v = got_ref[r, lo:lo + 208, :].astype(jnp.float32)
+            if o:
+                v = pltpu.roll(v, o, 1)
+            here = jnp.where(lane >= o, v, 0.0) if o > 32 else v
+            chunks[q] = here if chunks[q] is None else chunks[q] + here
+            if o > 32:
+                chunks[q + 1] = jnp.where(lane < o, v, 0.0)
+        for q in range(6):
+            ref[:, 128 * q:128 * q + 128] = chunks[q].astype(jnp.bfloat16)
+    r8 = lax.broadcasted_iota(jnp.int32, (8, 208), 0)
+    c8 = lax.broadcasted_iota(jnp.int32, (8, 208), 1)
+    pick = jnp.where((c8 < 200) & (c8 // F1 == r8), 1.0, 0.0).astype(jnp.bfloat16)
+    mean_one = jnp.dot(pick, xs[...], preferred_element_type=jnp.float32) / F1
+    ms[192:208, :] = jnp.concatenate([ms[192:208, :].astype(jnp.float32)[:8], mean_one], axis=0).astype(jnp.bfloat16)
+    rr = lax.broadcasted_iota(jnp.int32, (208, 8), 0)
+    cc = lax.broadcasted_iota(jnp.int32, (208, 8), 1)
+    spread = jnp.where(jnp.where(rr < 200, rr // F1, rr - 200) == cc, 1.0, 0.0)
+    ogs = jnp.dot(spread, og_ref[...].astype(jnp.float32), preferred_element_type=jnp.float32)
+    row = lax.broadcasted_iota(jnp.int32, (208, CP), 0)
+    og_one = jnp.where(row < 200, ogs, 0.0).astype(jnp.bfloat16)
+    og_seed = jnp.where(row < 200, 0.0, ogs).astype(jnp.bfloat16)
+    TN = (((0,), (0,)), ((), ()))
+    NT = (((1,), (1,)), ((), ()))
+
+    def grads(pair, put):
+        cols = pl.ds(pl.multiple_of(pair * WIDE, WIDE), WIDE)
+        pre = jnp.dot(xs[...], ws1[:, cols], preferred_element_type=jnp.float32) + jnp.dot(
+            ms[...], wn1[:, cols], preferred_element_type=jnp.float32)
+        s = 1.0 / (1.0 + jnp.exp(-pre))
+        h = (pre * s).astype(jnp.bfloat16)
+        d = lax.dot_general(og_one, wn2[cols, :], NT, preferred_element_type=jnp.float32) / F1 + lax.dot_general(
+            og_seed, ws2[cols, :], NT, preferred_element_type=jnp.float32)
+        g = (d * (s * (1.0 + pre * (1.0 - s)))).astype(jnp.bfloat16)
+        put(0, 768, lax.dot_general(xs[...], g, TN, preferred_element_type=jnp.float32))
+        put(768, 768, lax.dot_general(ms[...], g, TN, preferred_element_type=jnp.float32))
+        put(1536, CP, lax.dot_general(og_seed, h, TN, preferred_element_type=jnp.float32))
+        put(1536 + CP, CP, lax.dot_general(og_one, h, TN, preferred_element_type=jnp.float32) / F1)
+
+    waited = False
+    core_sem = [new(), new()]
+    for part in range(2):
+        def put(lo, n, v):
+            for c in range(2):
+                sib[part, c, lo:lo + n, :] = v[:, 128 * c:128 * c + 128].astype(jnp.bfloat16)
+        grads((1 - core) * 2 + part, put)
+        for c in range(2):
+            sib[part, c, 1536 + 2 * CP:, :] = jnp.zeros((ROWS_G - 1536 - 2 * CP, 128), jnp.bfloat16)
+        if not waited:
+            pl.semaphore_wait(barrier, len(peers))
+            waited = True
+        send(core_sem[part], sib.at[part], crecv.at[part], "c", 1)
+
+    def fold(part, row0, n, srcs):
+        step = min(n, 64)
+
+        def body(k, _):
+            o = pl.multiple_of(k * step, 16)
+            for c in range(2):
+                where = pl.ds(pl.multiple_of(row0 + o, 16), step)
+                v = acc[part, c, where, :]
+                for ref in srcs:
+                    v = v + ref[c, pl.ds(o, step), :].astype(jnp.float32)
+                acc[part, c, where, :] = v
+                sb[part, c, where, :] = v.astype(jnp.bfloat16)
+            return 0
+        lax.fori_loop(0, n // step, body, 0)
+
+    def rows(ref, part, row0, n):
+        return ref.at[part, :, pl.ds(pl.multiple_of(row0, 16), n)]
+
+    class Ring:
+        def __init__(self, part, axis, base, n, buf):
+            self.part, self.axis, self.base, self.n, self.buf = part, axis, base, n, buf
+            self.i = {"x": x, "y": y}[axis]
+            self.sem = [new() for _ in range(6)]
+
+        def q(self, k):
+            return self.base + self.n * ((self.i + k) % 4)
+
+        def go(self, m, row0, d):
+            send(self.sem[m], rows(sb, self.part, row0, self.n // 2), self.buf.at[self.part, m], self.axis, d)
+
+        def first(self):
+            h = self.n // 2
+            self.go(0, self.q(2), 1)
+            self.go(2, self.q(2) + h, -1)
+            self.go(1, self.q(1) + h, 1)
+            self.go(3, self.q(3), -1)
+
+        def second(self):
+            h = self.n // 2
+            for m, row0, d in ((0, self.q(1), 1), (2, self.q(3) + h, -1)):
+                arrive(self.sem[m], self.buf.at[self.part, m])
+                fold(self.part, row0, h, [self.buf.at[self.part, m]])
+                self.go(4 + m // 2, row0, d)
+
+        def last(self):
+            h = self.n // 2
+            for m in (3, 4, 1, 5):
+                arrive(self.sem[m], self.buf.at[self.part, m])
+            fold(self.part, self.q(0), h, [self.buf.at[self.part, 3], self.buf.at[self.part, 4]])
+            fold(self.part, self.q(0) + h, h, [self.buf.at[self.part, 1], self.buf.at[self.part, 5]])
+
+    axes = (("x", "y"), ("y", "x"))
+    rings1 = []
+    for part in range(2):
+        def put(lo, n, v):
+            for c in range(2):
+                acc[part, c, lo:lo + n, :] = v[:, 128 * c:128 * c + 128]
+        grads(core * 2 + part, put)
+        for c in range(2):
+            acc[part, c, 1536 + 2 * CP:, :] = jnp.zeros((ROWS_G - 1536 - 2 * CP, 128), jnp.float32)
+        arrive(core_sem[part], crecv.at[part])
+        fold(part, 0, ROWS_G, [crecv.at[part]])
+        ring = Ring(part, axes[part][0], 0, 512, big)
+        ring.first()
+        rings1.append(ring)
+    for ring in rings1:
+        ring.second()
+    rings2 = []
+    for ring in rings1:
+        ring.last()
+        nxt = Ring(ring.part, axes[ring.part][1], ring.q(0), 128, small)
+        nxt.first()
+        rings2.append(nxt)
+    for ring in rings2:
+        ring.second()
+    zsem = [[new() for _ in range(NZ - 1)] for _ in range(2)]
+    for ring in rings2:
+        ring.last()
+        for k in range(1, NZ):
+            send(zsem[ring.part][k - 1], rows(sb, ring.part, ring.q(0) + 16 * ((z + k) % NZ), 16), tiny.at[ring.part, k - 1], "z", k)
+
+    def final(part, row0, n):
+        return fin.at[pl.ds(4 * core + 2 * part, 2), pl.ds(pl.multiple_of(row0, 16), n)]
+
+    fsem = [[new() for _ in range(NZ - 1)] for _ in range(2)]
+    for ring in rings2:
+        p = ring.part
+        for k in range(1, NZ):
+            arrive(zsem[p][k - 1], tiny.at[p, k - 1])
+        r0 = pl.multiple_of(ring.q(0) + 16 * z, 16)
+        for c in range(2):
+            v = acc[p, c, pl.ds(r0, 16), :]
+            for k in range(NZ - 1):
+                v = v + tiny[p, k, c].astype(jnp.float32)
+            fin[4 * core + 2 * p + c, pl.ds(r0, 16), :] = v.astype(jnp.bfloat16)
+        for k in range(1, NZ):
+            here = final(p, r0, 16)
+            send(fsem[p][k - 1], here, here, "z", k)
+
+    def spread_first(part, axis, base, n, i, sem):
+        here = final(part, base + n * i, n)
+        send(sem[0], here, here, axis, 1)
+        send(sem[1], here, here, axis, -1)
+
+    def spread_second(part, axis, base, n, i, sem):
+        h = n // 2
+        a = base + n * ((i + 3) % 4)
+        arrive(sem[0], final(part, a, n))
+        here = final(part, a, h)
+        send(sem[2], here, here, axis, 1)
+        b = base + n * ((i + 1) % 4)
+        arrive(sem[1], final(part, b, n))
+        here = final(part, b + h, h)
+        send(sem[3], here, here, axis, -1)
+        return a, b
+
+    def spread_last(part, axis, base, n, i, sem):
+        o = base + n * ((i + 2) % 4)
+        arrive(sem[2], final(part, o, n // 2))
+        arrive(sem[3], final(part, o + n // 2, n // 2))
+        return o
+
+    sems = [[new() for _ in range(4)] for _ in range(2)]
+    for ring in rings2:
+        for k in range(1, NZ):
+            arrive(fsem[ring.part][k - 1], final(ring.part, ring.q(0) + 16 * ((z - k + NZ) % NZ), 16))
+        spread_first(ring.part, ring.axis, ring.base, 128, ring.i, sems[ring.part])
+    for ring in rings2:
+        spread_second(ring.part, ring.axis, ring.base, 128, ring.i, sems[ring.part])
+    sems1 = [[new() for _ in range(4)] for _ in range(2)]
+    csem = [[new() for _ in range(4)] for _ in range(2)]
+
+    def across(part, k, row0):
+        here = final(part, row0, 512)
+        send(csem[part][k], here, here, "c", 1)
+
+    for ring in rings2:
+        p = ring.part
+        spread_last(p, ring.axis, ring.base, 128, ring.i, sems[p])
+        spread_first(p, axes[p][0], 0, 512, rings1[p].i, sems1[p])
+        across(p, 0, rings1[p].q(0))
+    for ring in rings1:
+        p = ring.part
+        a, b = spread_second(p, ring.axis, 0, 512, ring.i, sems1[p])
+        across(p, 1, a)
+        across(p, 2, b)
+    for ring in rings1:
+        p = ring.part
+        across(p, 3, spread_last(p, ring.axis, 0, 512, ring.i, sems1[p]))
+    for ring in rings1:
+        p = ring.part
+        for k, off in enumerate((0, 3, 1, 2)):
+            here = fin.at[pl.ds(4 * (1 - core) + 2 * p, 2), pl.ds(pl.multiple_of(ring.q(off), 16), 512)]
+            arrive(csem[p][k], here)
+    for c in sent:
+        c.wait_send()
+    assert counter[0] == N_SEM, counter[0]
+
+
+def step(got, ws1, wn1, ws2, wn2, og):
+    bf, f32 = jnp.bfloat16, jnp.float32
+    return pl.pallas_call(
+        step_kernel,
+        out_shape=jax.ShapeDtypeStruct((8, ROWS_G, 128), bf),
+        in_specs=[pl.BlockSpec(memory_space=pltpu.VMEM)] * 6,
+        out_specs=pl.BlockSpec(memory_space=pltpu.VMEM),
+        scratch_shapes=[
+            pltpu.VMEM((208, 768), bf), pltpu.VMEM((208, 768), bf),
+            pltpu.VMEM((2, 2, ROWS_G, 128), f32), pltpu.VMEM((2, 2, ROWS_G, 128), bf),
+            pltpu.VMEM((2, 2, ROWS_G, 128), bf), pltpu.VMEM((2, 2, ROWS_G, 128), bf),
+            pltpu.VMEM((2, 6, 2, 256, 128), bf), pltpu.VMEM((2, 6, 2, 64, 128), bf), pltpu.VMEM((2, 7, 2, 16, 128), bf),
+            pltpu.SemaphoreType.DMA((N_SEM,)), pltpu.SemaphoreType.DMA((N_SEM,)),
+        ],
+        compiler_params=pltpu.CompilerParams(collective_id=1, has_side_effects=True, vmem_limit_bytes=56 * 2**20),
+        cost_estimate=pl.CostEstimate(flops=3 * 10**9, bytes_accessed=2 * 10**7, transcendentals=0),
+        name="step",
+    )(got, ws1, wn1, ws2, wn2, og)
+
+
+def finish(fin):
+    def tall(lo):
+        return fin[:, lo:lo + 768, :].transpose(1, 0, 2).reshape(768, 1024)
+
+    def wide(lo):
+        return fin[:, lo:lo + 153, :].transpose(0, 2, 1).reshape(1024, 153)
+    return tall(0), tall(768), wide(1536), wide(1536 + CP)
+
+
+def update(got, ws1, wn1, ws2, wn2, og):
+    pad = lambda a: jnp.pad(a, ((0, 0), (0, CP - a.shape[1])))
+    return finish(step(got, ws1, wn1, pad(ws2), pad(wn2), pad(og)))
 
 
 def per_device(
     table, near_owner, near_row, far_owner, far_row, w_self1, w_neigh1, w_self2, w_neigh2, out_grad
 ):
-    seeds, hidden = 8, w_self1.shape[1]
     got = fetch(build_idx(near_owner, near_row, far_owner, far_row), table)
-    got = got[:, :, :W].transpose(1, 0, 2).reshape(416, REP * W)
-    mean_two, x_one, x_seed = got[:200], got[208:408], got[408:]
-    mean_one = (jnp.sum(x_one.reshape(seeds, F1, -1), axis=1, dtype=jnp.float32) / F1).astype(jnp.bfloat16)
-    x_all = got[208:]
-    m_all = jnp.concatenate([mean_two, mean_one], axis=0)
-    pre = jnp.dot(x_all, w_self1, preferred_element_type=jnp.float32) + jnp.dot(
-        m_all, w_neigh1, preferred_element_type=jnp.float32
-    )
-    h = jax.nn.silu(pre).astype(jnp.bfloat16)
-    h_seed = h[200:]
-    mean_h = (jnp.sum(h[:200].reshape(seeds, F1, hidden), axis=1, dtype=jnp.float32) / F1).astype(jnp.bfloat16)
-    grad_self2 = jnp.dot(h_seed.T, out_grad, preferred_element_type=jnp.float32)
-    grad_neigh2 = jnp.dot(mean_h.T, out_grad, preferred_element_type=jnp.float32)
-    d_seed = jnp.dot(out_grad, w_self2.T, preferred_element_type=jnp.float32)
-    d_mean = jnp.dot(out_grad, w_neigh2.T, preferred_element_type=jnp.float32)
-    d_all = jnp.concatenate([jnp.repeat(d_mean / F1, F1, axis=0), d_seed], axis=0)
-    g = (d_all * silu_slope(pre)).astype(jnp.bfloat16)
-    grad_self1 = jnp.dot(x_all.T, g, preferred_element_type=jnp.float32)
-    grad_neigh1 = jnp.dot(m_all.T, g, preferred_element_type=jnp.float32)
-    grads = lax.psum((grad_self1, grad_neigh1, grad_self2, grad_neigh2), ("node", "rep"))
-    return tuple(v.astype(jnp.bfloat16) for v in grads)
+    return update(got, w_self1, w_neigh1, w_self2, w_neigh2, out_grad)
 
 
 def solution(mesh):

time: 275 us -> 185 us (0.67)
  blocking collectives: 140 us -> 0 us
  Pallas kernels: 108 us -> 168 us
  matrix products: 15.6 us -> 0 us
  local copies, waits for them, and re-layouts: 6.87 us -> 13.5 us
    psum x1 -> x0, blocking collectives: 140 us -> none  [per_device(): lax.psum((grad_self1, grad_neigh1, grad_self2, grad_neigh2), ('node', 're...]
    pallas_call x0 -> x1, Pallas kernels: none -> 60.2 us  [step(): pl.pallas_call(step_kernel, out_shape=jax.ShapeDtypeStruct((8, ROWS_G, 12...]
    dot_general x8 -> x0, matrix products: 15.6 us -> none  [the longest x1 3.32 us: per_device(): grad_neigh1 = jnp.dot(m_all.T, g, preferred_element_type=jnp.float32)]
    unnamed x16 -> x17, local copies, waits for them, and re-layouts: 1.09 us -> 5.55 us
    transpose x1 -> x4, local copies, waits for them, and re-layouts: 1.21 us -> 5.05 us  [the longest x3 3.77 us: tall(): return fin[:, lo:lo + 768, :].transpose(1, 0, 2).reshape(768, 1024)]
where the time goes in v2:
time: 185 us
  Pallas kernels  168 us (91%)
  local copies, waits for them, and re-layouts  13.5 us (7%)
  other arithmetic  2.22 us (1%)
    pallas_call x1, Pallas kernels, fetch(): pl.pallas_call(fetch_kernel, out_shape=jax.ShapeDtypeStruct((REP, 416, 12...  108 us
    pallas_call x1, Pallas kernels, step(): pl.pallas_call(step_kernel, out_shape=jax.ShapeDtypeStruct((8, ROWS_G, 12...  60.2 us
    unnamed x17, local copies, waits for them, and re-layouts  5.55 us
    transpose x3, local copies, waits for them, and re-layouts, tall(): return fin[:, lo:lo + 768, :].transpose(1, 0, 2).reshape(768, 1024)  3.77 us

profile of v2, /device:TPU:1, one launch (start us, length us, event | category | flops | bytes accessed | tf_op | source)
XLA Modules:
  0.0 184.7 jit_solution(16872931444136089020)
XLA Ops:
  0.6 0.7 bitcast_add_fusion.1
  1.4 0.1 reshape.44
  1.5 0.7 bitcast_add_fusion
  2.2 0.1 reshape.36
  2.3 0.1 pad_add_fusion
  2.5 0.1 reshape.38
  2.6 0.1 slice_reduce_fusion
  2.7 0.7 fusion.idx_ref
  3.4 108.1 %fetch.1.got_ref = bf16[8,416,128]{2,1,0:T(8,128)(2,1)} custom-call(s32[32,128]{1,0:T(8,128)} %fusion.idx_ref, bf16[1536,768]{1,0:T(8,128)(2,1)} %table_ref.1), custom_call_target="tpu_custom_call" | custom-call | flops 1000000000 | bytes 10000000 | tf_op jit(solution)/shard_map/fetch/pallas_call | solution.py:177
  111.5 0.2 copy.55
  111.7 0.9 pad.16.ws2
  112.6 0.2 copy.56
  112.8 0.9 pad.17.wn2
  113.7 0.6 pad.18.og_ref
  114.3 60.2 %step.1 = bf16[8,2048,128]{2,1,0:T(8,128)(2,1)} custom-call(bf16[8,416,128]{2,1,0:T(8,128)(2,1)} %fetch.1.got_ref, bf16[768,1024]{1,0:T(8,128)(2,1)} %ws1.1, bf16[768,1024]{1,0:T(8,128)(2,1)} %wn1.1, bf16[1024,160]{1,0:T(8,128)(2,1)} %pad.16.ws2, bf16[1024,160]{1,0:T(8,128)(2,1)} %pad.17.wn2, bf16[8,160]{1,0:T(8,128)(2,1)} %pad.18.og_ref), custom_call_target="tpu_custom_call" | custom-call | flops 3000000000 | bytes 20000000 | tf_op jit(solution)/shard_map/step/pallas_call | solution.py:475
  174.5 1.3 slice_bitcast_fusion.2
  175.8 0.2 copy_bitcast_fusion
  176.1 0.8 copy.63
  176.9 0.8 copy.64
  177.7 1.4 slice_bitcast_fusion
  179.0 1.7 copy.57
  180.7 1.6 copy.61
  182.4 0.7 copy.58
  183.1 1.6 copy.62
  (13 shorter events, 0.2 us)
Async XLA Ops:
  3.4 108.1 %copy-start.1 = (bf16[1024,153]{0,1:T(8,128)(2,1)S(1)}, bf16[1024,153]{0,1:T(8,128)(2,1)}, u32[]{:S(2)}) copy-start(bf16[1024,153]{0,1:T(8,128)(2,1)} %param.17) | copy-start | bytes 940036
  111.5 1.1 copy-start.2
  111.7 2.0 %copy-start.3 = (bf16[8,153]{1,0:T(8,128)(2,1)S(1)}, bf16[8,153]{1,0:T(8,128)(2,1)}, u32[]{:S(2)}) copy-start(bf16[8,153]{1,0:T(8,128)(2,1)} %param.19) | copy-start | bytes 7348
  174.5 3.2 %copy-start = (bf16[8,2048,128]{2,1,0:T(8,128)(2,1)S(1)}, bf16[8,2048,128]{2,1,0:T(8,128)(2,1)}, u32[]{:S(2)}) copy-start(bf16[8,2048,128]{2,1,0:T(8,128)(2,1)} %step.1) | copy-start | bytes 12582916

commit v3 on v2

v3 whole, which is shorter than its diff:
```python
import jax
import jax.numpy as jnp
from jax import lax
from jax.experimental import pallas as pl
from jax.experimental.pallas import tpu as pltpu
from jax.sharding import PartitionSpec as P

MESH = pl.DeviceIdType.MESH
NZ, NX, REP = 8, 4, 8
ROWS, W = 1536, 96
F1, F2 = 25, 15
G4 = ROWS // 4
UNITS = ((0, 80), (80, 80), (160, 112), (272, 112))
WIDE = 256
ROWS_G = 2048
C = 153
GS2, GN2 = 1536, 1696
N_SEM = 2 + 2 * (6 + 6 + 7 + 7 + 4 + 4 + 4)
GROUPS = 5


def plan():
    msgs = []
    def hops(size, half):
        out = []
        for h in range(1, size // 2 + 1):
            for d in (1, -1):
                if 2 * h == size and (d == 1) != (half == 0):
                    continue
                out.append((h, d))
        return out
    for u in range(4):
        half = u % 2
        first, second = ("x", "z") if u < 2 else ("z", "x")
        size = {"x": NX, "z": NZ}
        reach = [(0, 0)]
        for h, d in hops(size[first], half):
            off = {first: -h * d, second: 0}
            msgs.append((h, u, off["x"], off["z"], first, d))
            reach.append((-h * d, h))
        for o, base in reach:
            for h, d in hops(size[second], half):
                off = {first: o, second: -h * d}
                msgs.append((base + h, u, off["x"], off["z"], second, d))
    msgs.sort(key=lambda m: m[0])
    return msgs


PLAN = plan()


def kernel(no_ref, nr_ref, fo_ref, fr_ref, table, ws1_h, wn1_h, ws2, wn2, og_ref, gs1, gn1, gs2, gn2,
           tw, land, t32, sums, ones, stage, got, idx_own, idx_land, idx_smem, ws1, wn1,
           xs, ms, sb, sib, crecv, big, small, tiny, fin,
           ag_send, ag_recv, isend, irecv, osend, orecv, send_sem, recv_sem, lsem):
    node, rep = lax.axis_index("node"), lax.axis_index("rep")
    z, x = node // NX, node % NX
    y, core = rep // 2, rep % 2
    window = pl.multiple_of(128 * jnp.minimum(3 * rep // 4, 4), 128)
    get_table = pltpu.make_async_copy(table.at[:, pl.ds(window, 256)], tw, lsem.at[0])
    get_table.start()
    get_ws1 = pltpu.make_async_copy(ws1_h, ws1, lsem.at[1])
    get_wn1 = pltpu.make_async_copy(wn1_h, wn1, lsem.at[2])
    get_ws1.start()
    get_wn1.start()

    def at(dx, dz):
        return ((z + dz + 2 * NZ) % NZ) * NX + (x + dx + 2 * NX) % NX

    def dev(axis, d):
        if axis == "x":
            return (at(d, 0), rep)
        if axis == "y":
            return (node, ((y + d + 4) % 4) * 2 + core)
        if axis == "z":
            return (at(0, d), rep)
        if axis == "rep":
            return (node, (rep + d) % REP)
        return (node, y * 2 + 1 - core)

    barrier = pltpu.get_barrier_semaphore()
    peers = [("x", 1), ("x", -1)] + [("z", k) for k in range(1, NZ)] + [("rep", k) for k in range(1, REP)]
    for axis, d in peers:
        pl.semaphore_signal(barrier, inc=1, device_id=dev(axis, d), device_id_type=MESH)

    far = fo_ref[...] * ROWS + fr_ref[...]
    near = no_ref[...] * ROWS + nr_ref[...]
    idx_own[...] = jnp.zeros_like(idx_own)
    for t in range(GROUPS):
        idx_own[t, :, 0:75] = far[:, 75 * t:75 * t + 75]
        idx_own[t, :, 75:80] = near[:, 1 + 5 * t:6 + 5 * t]
        idx_own[t, :, 80:81] = near[:, 0:1]

    c = lax.broadcasted_iota(jnp.int32, (256, 384), 0)
    d = lax.broadcasted_iota(jnp.int32, (256, 384), 1)
    j = d // 128
    hit = c == rep * W - window + j * 32 + d % 32
    group = jnp.where(hit, ((d // 32) % 4 - j + 4) % 4, -1)
    perms = [jnp.where(group == g, 1.0, 0.0).astype(jnp.bfloat16) for g in range(4)]
    get_table.wait()

    def pack(lo, n):
        acc = jnp.zeros((n, 384), jnp.float32)
        for g in range(4):
            acc = acc + jnp.dot(tw[g * G4 + lo:g * G4 + lo + n, :], perms[g], preferred_element_type=jnp.float32)
        land[node, lo:lo + n, :] = acc.astype(jnp.bfloat16)

    def slot(u, n):
        return land.at[n, pl.ds(UNITS[u][0], UNITS[u][1])]

    def ag_copy(m, i):
        _, u, ox, oz, axis, dr = m
        s = slot(u, at(ox + dr, oz) if axis == "x" else at(ox, oz + dr))
        return pltpu.make_async_remote_copy(src_ref=s, dst_ref=s, send_sem=ag_send.at[i], recv_sem=ag_recv.at[i],
                                            device_id=dev(axis, dr), device_id_type=MESH)

    def ag_arrival(m, i):
        s = slot(m[1], at(m[2], m[3]))
        return pltpu.make_async_remote_copy(src_ref=s, dst_ref=s, send_sem=ag_send.at[i], recv_sem=ag_recv.at[i],
                                            device_id=dev("rep", 1), device_id_type=MESH)

    lane = lax.broadcasted_iota(jnp.int32, (96, 128), 1) // 32

    def unpack(n, half):
        def body(i, _):
            r0 = pl.multiple_of(i * 96, 16)
            p = land[n, pl.ds(r0, 96), :].astype(jnp.float32)
            ps = [p[:, 128 * q:128 * q + 128] for q in range(3)]
            for g in range(4):
                s = jnp.where(lane == g, ps[0], jnp.where(lane == (g + 1) % 4, ps[1], jnp.where(lane == (g + 2) % 4, ps[2], 0.0)))
                if g:
                    s = pltpu.roll(s, 128 - 32 * g, 1)
                t32[pl.ds(pl.multiple_of(n * ROWS + g * G4 + r0, 16), 96), :] = s
            return 0
        lax.fori_loop(2 * half, 2 * half + 2, body, 0)

    started = set()

    def start_children(u, ox, oz):
        for i, m in enumerate(PLAN):
            if m[1] != u or i in started:
                continue
            sx, sz = (m[2] + m[5], m[3]) if m[4] == "x" else (m[2], m[3] + m[5])
            if (sx % NX, sz % NZ) == (ox % NX, oz % NZ):
                started.add(i)
                ag_copy(m, i).start()

    pack(0, 160)
    pl.semaphore_wait(barrier, len(peers))
    for u in (0, 1):
        start_children(u, 0, 0)
    pack(160, 224)
    for u in (2, 3):
        start_children(u, 0, 0)

    def icopy(k):
        return pltpu.make_async_remote_copy(src_ref=idx_own, dst_ref=idx_land.at[rep], send_sem=isend.at[k], recv_sem=irecv.at[k],
                                            device_id=dev("rep", k), device_id_type=MESH)
    for k in range(1, REP):
        icopy(k).start()
    idx_land[rep] = idx_own[...]
    work = [(0, 0, 0), (0, 0, 1)]
    for t in range(1, PLAN[-1][0] + 1):
        seen = []
        for i, m in enumerate(PLAN):
            if m[0] != t:
                continue
            ag_arrival(m, i).wait_recv()
            start_children(m[1], m[2], m[3])
            if (m[2] % NX, m[3] % NZ) not in seen:
                seen.append((m[2] % NX, m[3] % NZ))
            if work:
                ox, oz, half = work.pop(0)
                unpack(at(ox, oz), half)
        work += [(ox, oz, half) for ox, oz in seen for half in range(2)]
        if t == 2:
            for k in range(1, REP):
                icopy(k).wait_recv()
            to_smem = pltpu.make_async_copy(idx_land, idx_smem, lsem.at[3])
            to_smem.start()
    for ox, oz, half in work:
        unpack(at(ox, oz), half)
    to_smem.wait()

    def ocopy(k):
        return pltpu.make_async_remote_copy(src_ref=stage.at[k], dst_ref=got.at[rep], send_sem=osend.at[k], recv_sem=orecv.at[k],
                                            device_id=dev("rep", k), device_id_type=MESH)

    def arrived_slice(k):
        there = got.at[(rep - k + REP) % REP]
        return pltpu.make_async_remote_copy(src_ref=there, dst_ref=there, send_sem=osend.at[k], recv_sem=orecv.at[k],
                                            device_id=dev("rep", k), device_id_type=MESH)

    sums[200:208, :] = jnp.zeros((8, 128), jnp.float32)
    for k in list(range(1, REP)) + [0]:
        p = (rep + k) % REP

        def body(i, _):
            t = i // 4
            for half in range(2):
                b = i % 4 * 2 + half

                def row(q):
                    return t32[pl.ds(idx_smem[p, t, b, q], 1), :]
                for u in range(5):
                    rows = [row(u * F2 + q) for q in range(F2)]
                    while len(rows) > 1:
                        rows = [rows[a] + rows[a + 1] if a + 1 < len(rows) else rows[a] for a in range(0, len(rows), 2)]
                    sums[pl.ds(b * F1 + t * 5 + u, 1), :] = rows[0]
                    ones[pl.ds(b * F1 + t * 5 + u, 1), :] = row(75 + u)
            return 0
        lax.fori_loop(0, 4 * GROUPS, body, 0)
        for b in range(8):
            ones[pl.ds(200 + b, 1), :] = t32[pl.ds(idx_smem[p, 0, b, 80], 1), :]
        for h, part in ((0, sums[...] / F2), (1, ones[...])):
            if k:
                stage[k, 208 * h:208 * h + 208, :] = part.astype(jnp.bfloat16)
            else:
                got[rep, 208 * h:208 * h + 208, :] = part.astype(jnp.bfloat16)
        if k:
            ocopy(k).start()
    get_ws1.wait()
    get_wn1.wait()
    for k in range(1, REP):
        arrived_slice(k).wait_recv()
    counter = [0]

    def acc_row(part, c, row):
        return (2 * part + c) * ROWS_G + row

    def new():
        counter[0] += 1
        return counter[0] - 1

    def copy(i, src, dst, axis, d):
        return pltpu.make_async_remote_copy(src_ref=src, dst_ref=dst, send_sem=send_sem.at[i], recv_sem=recv_sem.at[i],
                                            device_id=dev(axis, d), device_id_type=MESH)
    sent = []

    def send(i, src, dst, axis, d):
        c = copy(i, src, dst, axis, d)
        c.start()
        sent.append(c)

    def arrive(i, dst):
        copy(i, dst, dst, "c", 1).wait_recv()

    for ref, lo in ((ms, 0), (xs, 208)):
        lane = lax.broadcasted_iota(jnp.int32, (208, 128), 1)
        chunks = [None] * 6
        for r in range(REP):
            q, o = 96 * r // 128, 96 * r % 128
            v = got[r, lo:lo + 208, :].astype(jnp.float32)
            if o:
                v = pltpu.roll(v, o, 1)
            here = jnp.where(lane >= o, v, 0.0) if o > 32 else v
            chunks[q] = here if chunks[q] is None else chunks[q] + here
            if o > 32:
                chunks[q + 1] = jnp.where(lane < o, v, 0.0)
        for q in range(6):
            ref[:, 128 * q:128 * q + 128] = chunks[q].astype(jnp.bfloat16)
    r8 = lax.broadcasted_iota(jnp.int32, (8, 208), 0)
    c8 = lax.broadcasted_iota(jnp.int32, (8, 208), 1)
    pick = jnp.where((c8 < 200) & (c8 // F1 == r8), 1.0, 0.0).astype(jnp.bfloat16)
    mean_one = jnp.dot(pick, xs[...], preferred_element_type=jnp.float32) / F1
    ms[192:208, :] = jnp.concatenate([ms[192:208, :].astype(jnp.float32)[:8], mean_one], axis=0).astype(jnp.bfloat16)
    rr = lax.broadcasted_iota(jnp.int32, (208, 8), 0)
    cc = lax.broadcasted_iota(jnp.int32, (208, 8), 1)
    spread = jnp.where(jnp.where(rr < 200, rr // F1, rr - 200) == cc, 1.0, 0.0)
    ogs = jnp.dot(spread, og_ref[...].astype(jnp.float32), preferred_element_type=jnp.float32)
    row = lax.broadcasted_iota(jnp.int32, (208, C), 0)
    og_one = jnp.where(row < 200, ogs, 0.0).astype(jnp.bfloat16)
    og_seed = jnp.where(row < 200, 0.0, ogs).astype(jnp.bfloat16)
    TN = (((0,), (0,)), ((), ()))

    def grads(pair, put):
        cols = pl.ds(pl.multiple_of(pair * WIDE, WIDE), WIDE)
        pre = jnp.dot(xs[...], ws1[:, cols], preferred_element_type=jnp.float32) + jnp.dot(
            ms[...], wn1[:, cols], preferred_element_type=jnp.float32)
        s = 1.0 / (1.0 + jnp.exp(-pre))
        h = (pre * s).astype(jnp.bfloat16)
        d = jnp.dot(og_one, wn2[:, cols], preferred_element_type=jnp.float32) / F1 + jnp.dot(
            og_seed, ws2[:, cols], preferred_element_type=jnp.float32)
        g = (d * (s * (1.0 + pre * (1.0 - s)))).astype(jnp.bfloat16)
        put(0, 768, lax.dot_general(xs[...], g, TN, preferred_element_type=jnp.float32))
        put(768, 768, lax.dot_general(ms[...], g, TN, preferred_element_type=jnp.float32))
        put(GS2, C, lax.dot_general(og_seed, h, TN, preferred_element_type=jnp.float32))
        put(GN2, C, lax.dot_general(og_one, h, TN, preferred_element_type=jnp.float32) / F1)

    core_sem = [new(), new()]
    for part in range(2):
        sib[part, :, GS2:, :] = jnp.zeros((2, ROWS_G - GS2, 128), jnp.bfloat16)

        def put(lo, n, v):
            for c in range(2):
                sib[part, c, lo:lo + n, :] = v[:, 128 * c:128 * c + 128].astype(jnp.bfloat16)
        grads((1 - core) * 2 + part, put)
        send(core_sem[part], sib.at[part], crecv.at[part], "c", 1)

    def fold(part, row0, n, srcs):
        step = min(n, 64)

        def body(k, _):
            o = pl.multiple_of(k * step, 16)
            for c in range(2):
                where = pl.ds(pl.multiple_of(row0 + o, 16), step)
                mine = pl.ds(pl.multiple_of(acc_row(part, c, row0 + o), 16), step)
                v = t32[mine, :]
                for ref in srcs:
                    v = v + ref[c, pl.ds(o, step), :].astype(jnp.float32)
                t32[mine, :] = v
                sb[part, c, where, :] = v.astype(jnp.bfloat16)
            return 0
        lax.fori_loop(0, n // step, body, 0)

    def rows(ref, part, row0, n):
        return ref.at[part, :, pl.ds(pl.multiple_of(row0, 16), n)]

    class Ring:
        def __init__(self, part, axis, base, n, buf):
            self.part, self.axis, self.base, self.n, self.buf = part, axis, base, n, buf
            self.i = {"x": x, "y": y}[axis]
            self.sem = [new() for _ in range(6)]

        def q(self, k):
            return self.base + self.n * ((self.i + k) % 4)

        def go(self, m, row0, d):
            send(self.sem[m], rows(sb, self.part, row0, self.n // 2), self.buf.at[self.part, m], self.axis, d)

        def first(self):
            h = self.n // 2
            self.go(0, self.q(2), 1)
            self.go(2, self.q(2) + h, -1)
            self.go(1, self.q(1) + h, 1)
            self.go(3, self.q(3), -1)

        def second(self):
            h = self.n // 2
            for m, row0, d in ((0, self.q(1), 1), (2, self.q(3) + h, -1)):
                arrive(self.sem[m], self.buf.at[self.part, m])
                fold(self.part, row0, h, [self.buf.at[self.part, m]])
                self.go(4 + m // 2, row0, d)

        def last(self):
            h = self.n // 2
            for m in (3, 4, 1, 5):
                arrive(self.sem[m], self.buf.at[self.part, m])
            fold(self.part, self.q(0), h, [self.buf.at[self.part, 3], self.buf.at[self.part, 4]])
            fold(self.part, self.q(0) + h, h, [self.buf.at[self.part, 1], self.buf.at[self.part, 5]])

    axes = (("x", "y"), ("y", "x"))
    rings1 = []
    for part in range(2):
        for c in range(2):
            t32[acc_row(part, c, GS2):acc_row(part, c, ROWS_G), :] = jnp.zeros((ROWS_G - GS2, 128), jnp.float32)

        def put(lo, n, v):
            for c in range(2):
                t32[acc_row(part, c, lo):acc_row(part, c, lo) + n, :] = v[:, 128 * c:128 * c + 128]
        grads(core * 2 + part, put)
        arrive(core_sem[part], crecv.at[part])
        fold(part, 0, ROWS_G, [crecv.at[part]])
        ring = Ring(part, axes[part][0], 0, 512, big)
        ring.first()
        rings1.append(ring)
    for ring in rings1:
        ring.second()
    rings2 = []
    for ring in rings1:
        ring.last()
        nxt = Ring(ring.part, axes[ring.part][1], ring.q(0), 128, small)
        nxt.first()
        rings2.append(nxt)
    for ring in rings2:
        ring.second()
    zsem = [[new() for _ in range(NZ - 1)] for _ in range(2)]
    for ring in rings2:
        ring.last()
        for k in range(1, NZ):
            send(zsem[ring.part][k - 1], rows(sb, ring.part, ring.q(0) + 16 * ((z + k) % NZ), 16), tiny.at[ring.part, k - 1], "z", k)

    def final(part, row0, n):
        return fin.at[pl.ds(4 * core + 2 * part, 2), pl.ds(pl.multiple_of(row0, 16), n)]

    fsem = [[new() for _ in range(NZ - 1)] for _ in range(2)]
    for ring in rings2:
        p = ring.part
        for k in range(1, NZ):
            arrive(zsem[p][k - 1], tiny.at[p, k - 1])
        r0 = pl.multiple_of(ring.q(0) + 16 * z, 16)
        for c in range(2):
            v = t32[pl.ds(pl.multiple_of(acc_row(p, c, r0), 16), 16), :]
            for k in range(NZ - 1):
                v = v + tiny[p, k, c].astype(jnp.float32)
            fin[4 * core + 2 * p + c, pl.ds(r0, 16), :] = v.astype(jnp.bfloat16)
        for k in range(1, NZ):
            here = final(p, r0, 16)
            send(fsem[p][k - 1], here, here, "z", k)

    def spread_first(part, axis, base, n, i, sem):
        here = final(part, base + n * i, n)
        send(sem[0], here, here, axis, 1)
        send(sem[1], here, here, axis, -1)

    def spread_second(part, axis, base, n, i, sem):
        h = n // 2
        a = base + n * ((i + 3) % 4)
        arrive(sem[0], final(part, a, n))
        here = final(part, a, h)
        send(sem[2], here, here, axis, 1)
        b = base + n * ((i + 1) % 4)
        arrive(sem[1], final(part, b, n))
        here = final(part, b + h, h)
        send(sem[3], here, here, axis, -1)
        return a, b

    def spread_last(part, axis, base, n, i, sem):
        o = base + n * ((i + 2) % 4)
        arrive(sem[2], final(part, o, n // 2))
        arrive(sem[3], final(part, o + n // 2, n // 2))
        return o

    sems = [[new() for _ in range(4)] for _ in range(2)]
    for ring in rings2:
        for k in range(1, NZ):
            arrive(fsem[ring.part][k - 1], final(ring.part, ring.q(0) + 16 * ((z - k + NZ) % NZ), 16))
        spread_first(ring.part, ring.axis, ring.base, 128, ring.i, sems[ring.part])
    for ring in rings2:
        spread_second(ring.part, ring.axis, ring.base, 128, ring.i, sems[ring.part])
    sems1 = [[new() for _ in range(4)] for _ in range(2)]
    csem = [[new() for _ in range(4)] for _ in range(2)]

    def across(part, k, row0):
        here = final(part, row0, 512)
        send(csem[part][k], here, here, "c", 1)

    for ring in rings2:
        p = ring.part
        spread_last(p, ring.axis, ring.base, 128, ring.i, sems[p])
        spread_first(p, axes[p][0], 0, 512, rings1[p].i, sems1[p])
        across(p, 0, rings1[p].q(0))
    for ring in rings1:
        p = ring.part
        a, b = spread_second(p, ring.axis, 0, 512, ring.i, sems1[p])
        across(p, 1, a)
        across(p, 2, b)
    for ring in rings1:
        p = ring.part
        across(p, 3, spread_last(p, ring.axis, 0, 512, ring.i, sems1[p]))
    for ring in rings1:
        p = ring.part
        for k, off in enumerate((0, 3, 1, 2)):
            here = fin.at[pl.ds(4 * (1 - core) + 2 * p, 2), pl.ds(pl.multiple_of(ring.q(off), 16), 512)]
            arrive(csem[p][k], here)
    outs = []
    for h in range(8):
        for n, (ref, lo) in enumerate(((gs1, 0), (gn1, 768))):
            outs.append(pltpu.make_async_copy(fin.at[h, pl.ds(lo, 768)], ref.at[:, pl.ds(128 * h, 128)], lsem.at[4 + 2 * h + n]))
            outs[-1].start()
    for h in range(8):
        for ref, lo in ((gs2, GS2), (gn2, GN2)):
            ref[:, 128 * h:128 * h + 128] = fin[h, lo:lo + C, :]
    for c in outs:
        c.wait()
    for c in sent:
        c.wait_send()
    for k in range(1, REP):
        ocopy(k).wait_send()
        icopy(k).wait_send()
    for i, m in enumerate(PLAN):
        ag_copy(m, i).wait_send()
    assert counter[0] == N_SEM, counter[0]


def per_device(
    table, near_owner, near_row, far_owner, far_row, w_self1, w_neigh1, w_self2, w_neigh2, out_grad
):
    bf, f32, n = jnp.bfloat16, jnp.float32, len(PLAN)
    vmem, hbm, dma = pl.BlockSpec(memory_space=pltpu.VMEM), pl.BlockSpec(memory_space=pl.ANY), pltpu.SemaphoreType.DMA
    turned = [w_self2.T, w_neigh2.T]
    out = pl.pallas_call(
        kernel,
        out_shape=[jax.ShapeDtypeStruct(a.shape, bf) for a in (w_self1, w_neigh1, *turned)],
        in_specs=[vmem] * 4 + [hbm] * 3 + [vmem] * 3,
        out_specs=[hbm, hbm, vmem, vmem],
        scratch_shapes=[
            pltpu.VMEM((ROWS, 256), bf),
            pltpu.VMEM((NZ * NX, G4, 384), bf),
            pltpu.VMEM((NZ * NX * ROWS, 128), f32),
            pltpu.VMEM((208, 128), f32),
            pltpu.VMEM((208, 128), f32),
            pltpu.VMEM((REP, 416, 128), bf),
            pltpu.VMEM((REP, 416, 128), bf),
            pltpu.VMEM((GROUPS, 8, 128), jnp.int32),
            pltpu.VMEM((REP, GROUPS, 8, 128), jnp.int32),
            pltpu.SMEM((REP, GROUPS, 8, 128), jnp.int32),
            pltpu.VMEM((768, 1024), bf),
            pltpu.VMEM((768, 1024), bf),
            pltpu.VMEM((208, 768), bf),
            pltpu.VMEM((208, 768), bf),
            pltpu.VMEM((2, 2, ROWS_G, 128), bf),
            pltpu.VMEM((2, 2, ROWS_G, 128), bf),
            pltpu.VMEM((2, 2, ROWS_G, 128), bf),
            pltpu.VMEM((2, 6, 2, 256, 128), bf),
            pltpu.VMEM((2, 6, 2, 64, 128), bf),
            pltpu.VMEM((2, 7, 2, 16, 128), bf),
            pltpu.VMEM((8, ROWS_G, 128), bf),
            dma((n,)), dma((n,)), dma((REP,)), dma((REP,)), dma((REP,)), dma((REP,)), dma((N_SEM,)), dma((N_SEM,)), dma((20,)),
        ],
        compiler_params=pltpu.CompilerParams(collective_id=0, has_side_effects=True, vmem_limit_bytes=61 * 10**6),
        cost_estimate=pl.CostEstimate(flops=4 * 10**9, bytes_accessed=3 * 10**7, transcendentals=0),
        name="step",
    )(near_owner.reshape(near_row.shape), near_row, far_owner.reshape(far_row.shape), far_row, table,
      w_self1, w_neigh1, *turned, out_grad)
    return out[0], out[1], out[2].T, out[3].T


def solution(mesh):
    rows = P(("node", "rep"))
    return jax.shard_map(
        per_device,
        mesh=mesh,
        in_specs=(P("node"), rows, rows, rows, rows, P(), P(), P(), P(), rows),
        out_specs=(P(), P(), P(), P()),
        check_vma=False,
    )
```

time: 185 us -> 162 us (0.88)
  Pallas kernels: 168 us -> 155 us
  local copies, waits for them, and re-layouts: 13.5 us -> 6.71 us
  other arithmetic: 2.22 us -> 0 us
    pallas_call x2 -> x1, Pallas kernels: 168 us -> 155 us  [per_device(): pl.pallas_call(kernel, out_shape=[jax.ShapeDtypeStruct(a.shape, bf) for a...]
    transpose x4 -> x0, local copies, waits for them, and re-layouts: 5.05 us -> none  [the longest x3 3.77 us: tall(): return fin[:, lo:lo + 768, :].transpose(1, 0, 2).reshape(768, 1024)]
    pad x3 -> x0, local copies, waits for them, and re-layouts: 2.37 us -> none  [update(): pad = lambda a: jnp.pad(a, ((0, 0), (0, CP - a.shape[1])))]
    unnamed x17 -> x11, local copies, waits for them, and re-layouts: 5.55 us -> 6.71 us
where the time goes in v3:
time: 162 us
  Pallas kernels  155 us (96%)
  local copies, waits for them, and re-layouts  6.71 us (4%)
    pallas_call x1, Pallas kernels, per_device(): pl.pallas_call(kernel, out_shape=[jax.ShapeDtypeStruct(a.shape, bf) for a...  155 us
    unnamed x11, local copies, waits for them, and re-layouts  6.71 us

profile of v3, /device:TPU:1, one launch (start us, length us, event | category | flops | bytes accessed | tf_op | source)
XLA Modules:
  0.0 162.0 jit_solution(18053758533009503986)
XLA Ops:
  0.6 1.3 copy.16
  1.9 154.7 %step.1 = (bf16[768,1024]{1,0:T(8,128)(2,1)}, bf16[768,1024]{1,0:T(8,128)(2,1)}, bf16[153,1024]{1,0:T(8,128)(2,1)}, bf16[153,1024]{1,0:T(8,128)(2,1)}) custom-call(s32[8,26]{1,0:T(8,128)} %bitcast.13, s32[8,26]{1,0:T(8,128)} %nr_ref.1, s32[8,375]{1,0:T(8,128)} %bitcast.10, s32[8,375]{1,0:T(8,128)} %fr_ref.1, bf16[1536,768]{1,0:T(8,128)(2,1)} %table.1, ...), custom_call_target="tpu_custom_call" | custom-call | flops 4000000000 | bytes 30000000 | tf_op jit(solution)/shard_map/step/pallas_call | solution.py:482
  156.6 0.0 copy-start
  156.6 2.8 %copy.21 = bf16[768,1024]{1,0:T(8,128)(2,1)} copy(bf16[768,1024]{1,0:T(8,128)(2,1)} %get-tuple-element.16) | data formatting | bytes 3145728
  159.4 0.0 copy-done
  159.4 0.0 copy-start.2
  159.4 0.0 copy-start.1
  159.4 1.1 copy.22
  160.6 0.0 copy-done.2
  160.6 0.7 copy.23
  161.3 0.0 copy-done.1
  161.3 0.7 copy.24
Async XLA Ops:
  156.6 2.8 %copy-start = (bf16[768,1024]{1,0:T(8,128)(2,1)S(1)}, bf16[768,1024]{1,0:T(8,128)(2,1)}, u32[]{:S(2)}) copy-start(bf16[768,1024]{1,0:T(8,128)(2,1)} %get-tuple-element.17) | copy-start | bytes 4718596
  159.4 1.2 copy-start.2
  159.4 1.9 %copy-start.1 = (bf16[153,1024]{1,0:T(8,128)(2,1)S(1)}, bf16[153,1024]{1,0:T(8,128)(2,1)}, u32[]{:S(2)}) copy-start(bf16[153,1024]{1,0:T(8,128)(2,1)} %get-tuple-element.11) | copy-start | bytes 940036

commit v4 on v3

--- a/solution.py
+++ b/solution.py
@@ -15,7 +15,8 @@
 ROWS_G = 2048
 C = 153
 GS2, GN2 = 1536, 1696
-N_SEM = 2 + 2 * (6 + 6 + 7 + 7 + 4 + 4 + 4)
+PARTS = 4
+N_SEM = PARTS * (1 + 6 + 6 + 7 + 7 + 4 + 4 + 4)
 GROUPS = 5
 
 
@@ -225,8 +226,8 @@
         arrived_slice(k).wait_recv()
     counter = [0]
 
-    def acc_row(part, c, row):
-        return (2 * part + c) * ROWS_G + row
+    def acc_row(part, row):
+        return part * ROWS_G + row
 
     def new():
         counter[0] += 1
@@ -287,34 +288,34 @@
         put(GS2, C, lax.dot_general(og_seed, h, TN, preferred_element_type=jnp.float32))
         put(GN2, C, lax.dot_general(og_one, h, TN, preferred_element_type=jnp.float32) / F1)
 
-    core_sem = [new(), new()]
-    for part in range(2):
-        sib[part, :, GS2:, :] = jnp.zeros((2, ROWS_G - GS2, 128), jnp.bfloat16)
+    core_sem = [new() for _ in range(PARTS)]
+    for pair in range(2):
+        parts = (2 * pair, 2 * pair + 1)
+        sib[2 * pair:2 * pair + 2, GS2:, :] = jnp.zeros((2, ROWS_G - GS2, 128), jnp.bfloat16)
 
         def put(lo, n, v):
             for c in range(2):
-                sib[part, c, lo:lo + n, :] = v[:, 128 * c:128 * c + 128].astype(jnp.bfloat16)
-        grads((1 - core) * 2 + part, put)
-        send(core_sem[part], sib.at[part], crecv.at[part], "c", 1)
+                sib[parts[c], lo:lo + n, :] = v[:, 128 * c:128 * c + 128].astype(jnp.bfloat16)
+        grads((1 - core) * 2 + pair, put)
+        for p in parts:
+            send(core_sem[p], sib.at[p], crecv.at[p], "c", 1)
 
     def fold(part, row0, n, srcs):
-        step = min(n, 64)
+        step = min(n, 128)
 
         def body(k, _):
             o = pl.multiple_of(k * step, 16)
-            for c in range(2):
-                where = pl.ds(pl.multiple_of(row0 + o, 16), step)
-                mine = pl.ds(pl.multiple_of(acc_row(part, c, row0 + o), 16), step)
-                v = t32[mine, :]
-                for ref in srcs:
-                    v = v + ref[c, pl.ds(o, step), :].astype(jnp.float32)
-                t32[mine, :] = v
-                sb[part, c, where, :] = v.astype(jnp.bfloat16)
+            mine = pl.ds(pl.multiple_of(acc_row(part, row0 + o), 16), step)
+            v = t32[mine, :]
+            for ref in srcs:
+                v = v + ref[pl.ds(o, step), :].astype(jnp.float32)
+            t32[mine, :] = v
+            sb[part, pl.ds(pl.multiple_of(row0 + o, 16), step), :] = v.astype(jnp.bfloat16)
             return 0
         lax.fori_loop(0, n // step, body, 0)
 
     def rows(ref, part, row0, n):
-        return ref.at[part, :, pl.ds(pl.multiple_of(row0, 16), n)]
+        return ref.at[part, pl.ds(pl.multiple_of(row0, 16), n)]
 
     class Ring:
         def __init__(self, part, axis, base, n, buf):
@@ -349,21 +350,23 @@
             fold(self.part, self.q(0), h, [self.buf.at[self.part, 3], self.buf.at[self.part, 4]])
             fold(self.part, self.q(0) + h, h, [self.buf.at[self.part, 1], self.buf.at[self.part, 5]])
 
-    axes = (("x", "y"), ("y", "x"))
+    axes = (("x", "y"), ("y", "x")) * (PARTS // 2)
     rings1 = []
-    for part in range(2):
-        for c in range(2):
-            t32[acc_row(part, c, GS2):acc_row(part, c, ROWS_G), :] = jnp.zeros((ROWS_G - GS2, 128), jnp.float32)
+    for pair in range(2):
+        parts = (2 * pair, 2 * pair + 1)
+        for p in parts:
+            t32[acc_row(p, GS2):acc_row(p, ROWS_G), :] = jnp.zeros((ROWS_G - GS2, 128), jnp.float32)
 
         def put(lo, n, v):
             for c in range(2):
-                t32[acc_row(part, c, lo):acc_row(part, c, lo) + n, :] = v[:, 128 * c:128 * c + 128]
-        grads(core * 2 + part, put)
-        arrive(core_sem[part], crecv.at[part])
-        fold(part, 0, ROWS_G, [crecv.at[part]])
-        ring = Ring(part, axes[part][0], 0, 512, big)
-        ring.first()
-        rings1.append(ring)
+                t32[acc_row(parts[c], lo):acc_row(parts[c], lo) + n, :] = v[:, 128 * c:128 * c + 128]
+        grads(core * 2 + pair, put)
+        for p in parts:
+            arrive(core_sem[p], crecv.at[p])
+            fold(p, 0, ROWS_G, [crecv.at[p]])
+            ring = Ring(p, axes[p][0], 0, 512, big)
+            ring.first()
+            rings1.append(ring)
     for ring in rings1:
         ring.second()
     rings2 = []
@@ -374,26 +377,25 @@
         rings2.append(nxt)
     for ring in rings2:
         ring.second()
-    zsem = [[new() for _ in range(NZ - 1)] for _ in range(2)]
+    zsem = [[new() for _ in range(NZ - 1)] for _ in range(PARTS)]
     for ring in rings2:
         ring.last()
         for k in range(1, NZ):
             send(zsem[ring.part][k - 1], rows(sb, ring.part, ring.q(0) + 16 * ((z + k) % NZ), 16), tiny.at[ring.part, k - 1], "z", k)
 
     def final(part, row0, n):
-        return fin.at[pl.ds(4 * core + 2 * part, 2), pl.ds(pl.multiple_of(row0, 16), n)]
-
-    fsem = [[new() for _ in range(NZ - 1)] for _ in range(2)]
+        return fin.at[4 * core + part, pl.ds(pl.multiple_of(row0, 16), n)]
+
+    fsem = [[new() for _ in range(NZ - 1)] for _ in range(PARTS)]
     for ring in rings2:
         p = ring.part
         for k in range(1, NZ):
             arrive(zsem[p][k - 1], tiny.at[p, k - 1])
         r0 = pl.multiple_of(ring.q(0) + 16 * z, 16)
-        for c in range(2):
-            v = t32[pl.ds(pl.multiple_of(acc_row(p, c, r0), 16), 16), :]
-            for k in range(NZ - 1):
-                v = v + tiny[p, k, c].astype(jnp.float32)
-            fin[4 * core + 2 * p + c, pl.ds(r0, 16), :] = v.astype(jnp.bfloat16)
+        v = t32[pl.ds(pl.multiple_of(acc_row(p, r0), 16), 16), :]
+        for k in range(NZ - 1):
+            v = v + tiny[p, k].astype(jnp.float32)
+        fin[4 * core + p, pl.ds(r0, 16), :] = v.astype(jnp.bfloat16)
         for k in range(1, NZ):
             here = final(p, r0, 16)
             send(fsem[p][k - 1], here, here, "z", k)
@@ -421,15 +423,15 @@
         arrive(sem[3], final(part, o + n // 2, n // 2))
         return o
 
-    sems = [[new() for _ in range(4)] for _ in range(2)]
+    sems = [[new() for _ in range(4)] for _ in range(PARTS)]
     for ring in rings2:
         for k in range(1, NZ):
             arrive(fsem[ring.part][k - 1], final(ring.part, ring.q(0) + 16 * ((z - k + NZ) % NZ), 16))
         spread_first(ring.part, ring.axis, ring.base, 128, ring.i, sems[ring.part])
     for ring in rings2:
         spread_second(ring.part, ring.axis, ring.base, 128, ring.i, sems[ring.part])
-    sems1 = [[new() for _ in range(4)] for _ in range(2)]
-    csem = [[new() for _ in range(4)] for _ in range(2)]
+    sems1 = [[new() for _ in range(4)] for _ in range(PARTS)]
+    csem = [[new() for _ in range(4)] for _ in range(PARTS)]
 
     def across(part, k, row0):
         here = final(part, row0, 512)
@@ -451,7 +453,7 @@
     for ring in rings1:
         p = ring.part
         for k, off in enumerate((0, 3, 1, 2)):
-            here = fin.at[pl.ds(4 * (1 - core) + 2 * p, 2), pl.ds(pl.multiple_of(ring.q(off), 16), 512)]
+            here = fin.at[4 * (1 - core) + p, pl.ds(pl.multiple_of(ring.q(off), 16), 512)]
             arrive(csem[p][k], here)
     outs = []
     for h in range(8):
@@ -499,12 +501,12 @@
             pltpu.VMEM((768, 1024), bf),
             pltpu.VMEM((208, 768), bf),
             pltpu.VMEM((208, 768), bf),
-            pltpu.VMEM((2, 2, ROWS_G, 128), bf),
-            pltpu.VMEM((2, 2, ROWS_G, 128), bf),
-            pltpu.VMEM((2, 2, ROWS_G, 128), bf),
-            pltpu.VMEM((2, 6, 2, 256, 128), bf),
-            pltpu.VMEM((2, 6, 2, 64, 128), bf),
-            pltpu.VMEM((2, 7, 2, 16, 128), bf),
+            pltpu.VMEM((PARTS, ROWS_G, 128), bf),
+            pltpu.VMEM((PARTS, ROWS_G, 128), bf),
+            pltpu.VMEM((PARTS, ROWS_G, 128), bf),
+            pltpu.VMEM((PARTS, 6, 256, 128), bf),
+            pltpu.VMEM((PARTS, 6, 64, 128), bf),
+            pltpu.VMEM((PARTS, 7, 16, 128), bf),
             pltpu.VMEM((8, ROWS_G, 128), bf),
             dma((n,)), dma((n,)), dma((REP,)), dma((REP,)), dma((REP,)), dma((REP,)), dma((N_SEM,)), dma((N_SEM,)), dma((20,)),
         ],

time: 162 us -> 160 us (0.988)
  Pallas kernels: 155 us -> 152 us
    pallas_call x1, Pallas kernels: 155 us -> 152 us  [per_device(): pl.pallas_call(kernel, out_shape=[jax.ShapeDtypeStruct(a.shape, bf) for a...]
where the time goes in v4:
time: 160 us
  Pallas kernels  152 us (95%)
  local copies, waits for them, and re-layouts  6.71 us (4%)
    pallas_call x1, Pallas kernels, per_device(): pl.pallas_call(kernel, out_shape=[jax.ShapeDtypeStruct(a.shape, bf) for a...  152 us
    unnamed x11, local copies, waits for them, and re-layouts  6.71 us

profile of v4, /device:TPU:1, one launch (start us, length us, event | category | flops | bytes accessed | tf_op | source)
XLA Modules:
  0.0 159.6 jit_solution(17063882447180539622)
XLA Ops:
  0.6 1.3 copy.16
  1.9 152.2 %step.1 = (bf16[768,1024]{1,0:T(8,128)(2,1)}, bf16[768,1024]{1,0:T(8,128)(2,1)}, bf16[153,1024]{1,0:T(8,128)(2,1)}, bf16[153,1024]{1,0:T(8,128)(2,1)}) custom-call(s32[8,26]{1,0:T(8,128)} %bitcast.13, s32[8,26]{1,0:T(8,128)} %nr_ref.1, s32[8,375]{1,0:T(8,128)} %bitcast.10, s32[8,375]{1,0:T(8,128)} %fr_ref.1, bf16[1536,768]{1,0:T(8,128)(2,1)} %table.1, ...), custom_call_target="tpu_custom_call" | custom-call | flops 4000000000 | bytes 30000000 | tf_op jit(solution)/shard_map/step/pallas_call | solution.py:484
  154.2 0.0 copy-start
  154.2 2.8 %copy.21 = bf16[768,1024]{1,0:T(8,128)(2,1)} copy(bf16[768,1024]{1,0:T(8,128)(2,1)} %get-tuple-element.16) | data formatting | bytes 3145728
  157.0 0.0 copy-done
  157.0 0.0 copy-start.2
  157.0 0.0 copy-start.1
  157.0 1.1 copy.22
  158.1 0.0 copy-done.2
  158.1 0.7 copy.23
  158.9 0.0 copy-done.1
  158.9 0.7 copy.24
Async XLA Ops:
  154.2 2.8 %copy-start = (bf16[768,1024]{1,0:T(8,128)(2,1)S(1)}, bf16[768,1024]{1,0:T(8,128)(2,1)}, u32[]{:S(2)}) copy-start(bf16[768,1024]{1,0:T(8,128)(2,1)} %get-tuple-element.17) | copy-start | bytes 4718596
  157.0 1.2 copy-start.2
  157.0 1.9 %copy-start.1 = (bf16[153,1024]{1,0:T(8,128)(2,1)S(1)}, bf16[153,1024]{1,0:T(8,128)(2,1)}, u32[]{:S(2)}) copy-start(bf16[153,1024]{1,0:T(8,128)(2,1)} %get-tuple-element.11) | copy-start | bytes 940036

commit v5 on v4

--- a/solution.py
+++ b/solution.py
@@ -450,19 +450,25 @@
     for ring in rings1:
         p = ring.part
         across(p, 3, spread_last(p, ring.axis, 0, 512, ring.i, sems1[p]))
+    outs = []
+
+    def deliver(n, h):
+        cols = pl.ds(pl.multiple_of(128 * h, 128), 128)
+        for m, (ref, lo) in enumerate(((gs1, 0), (gn1, 768))):
+            outs.append(pltpu.make_async_copy(fin.at[h, pl.ds(lo, 768)], ref.at[:, cols], lsem.at[4 + 2 * n + m]))
+            outs[-1].start()
+        for ref, lo in ((gs2, GS2), (gn2, GN2)):
+            ref[:, cols] = fin[h, lo:lo + C, :]
+
+    for p in range(PARTS):
+        deliver(p, 4 * core + p)
     for ring in rings1:
         p = ring.part
         for k, off in enumerate((0, 3, 1, 2)):
             here = fin.at[4 * (1 - core) + p, pl.ds(pl.multiple_of(ring.q(off), 16), 512)]
             arrive(csem[p][k], here)
-    outs = []
-    for h in range(8):
-        for n, (ref, lo) in enumerate(((gs1, 0), (gn1, 768))):
-            outs.append(pltpu.make_async_copy(fin.at[h, pl.ds(lo, 768)], ref.at[:, pl.ds(128 * h, 128)], lsem.at[4 + 2 * h + n]))
-            outs[-1].start()
-    for h in range(8):
-        for ref, lo in ((gs2, GS2), (gn2, GN2)):
-            ref[:, 128 * h:128 * h + 128] = fin[h, lo:lo + C, :]
+        deliver(PARTS + p, 4 * (1 - core) + p)
+    assert counter[0] == N_SEM, counter[0]
     for c in outs:
         c.wait()
     for c in sent:
@@ -472,7 +478,6 @@
         icopy(k).wait_send()
     for i, m in enumerate(PLAN):
         ag_copy(m, i).wait_send()
-    assert counter[0] == N_SEM, counter[0]
 
 
 def per_device(

time: 160 us -> 159 us (level)
  no operation moved by 1% of the time
where the time goes in v5:
time: 159 us
  Pallas kernels  151 us (95%)
  local copies, waits for them, and re-layouts  6.71 us (4%)
    pallas_call x1, Pallas kernels, per_device(): pl.pallas_call(kernel, out_shape=[jax.ShapeDtypeStruct(a.shape, bf) for a...  151 us
    unnamed x11, local copies, waits for them, and re-layouts  6.71 us

profile of v5, /device:TPU:1, one launch (start us, length us, event | category | flops | bytes accessed | tf_op | source)
XLA Modules:
  0.0 158.6 jit_solution(15149706135589623578)
XLA Ops:
  0.6 1.3 copy.16
  1.9 151.3 %step.1 = (bf16[768,1024]{1,0:T(8,128)(2,1)}, bf16[768,1024]{1,0:T(8,128)(2,1)}, bf16[153,1024]{1,0:T(8,128)(2,1)}, bf16[153,1024]{1,0:T(8,128)(2,1)}) custom-call(s32[8,26]{1,0:T(8,128)} %bitcast.13, s32[8,26]{1,0:T(8,128)} %nr_ref.1, s32[8,375]{1,0:T(8,128)} %bitcast.10, s32[8,375]{1,0:T(8,128)} %fr_ref.1, bf16[1536,768]{1,0:T(8,128)(2,1)} %table.1, ...), custom_call_target="tpu_custom_call" | custom-call | flops 4000000000 | bytes 30000000 | tf_op jit(solution)/shard_map/step/pallas_call | solution.py:489
  153.2 0.0 copy-start
  153.2 2.8 %copy.21 = bf16[768,1024]{1,0:T(8,128)(2,1)} copy(bf16[768,1024]{1,0:T(8,128)(2,1)} %get-tuple-element.16) | data formatting | bytes 3145728
  156.0 0.0 copy-done
  156.0 0.0 copy-start.2
  156.0 0.0 copy-start.1
  156.0 1.1 copy.22
  157.2 0.0 copy-done.2
  157.2 0.7 copy.23
  157.9 0.0 copy-done.1
  157.9 0.7 copy.24
Async XLA Ops:
  153.2 2.8 %copy-start = (bf16[768,1024]{1,0:T(8,128)(2,1)S(1)}, bf16[768,1024]{1,0:T(8,128)(2,1)}, u32[]{:S(2)}) copy-start(bf16[768,1024]{1,0:T(8,128)(2,1)} %get-tuple-element.17) | copy-start | bytes 4718596
  156.0 1.2 copy-start.2
  156.0 1.9 %copy-start.1 = (bf16[153,1024]{1,0:T(8,128)(2,1)S(1)}, bf16[153,1024]{1,0:T(8,128)(2,1)}, u32[]{:S(2)}) copy-start(bf16[153,1024]{1,0:T(8,128)(2,1)} %get-tuple-element.11) | copy-start | bytes 940036
